TPU v7x, 32 devices: a whole 2x2x4 slice. The times are simulated.
32 devices in a mesh: groups: 2 (over x), dp: 8 (over z, y), tensor: 2 (over core).
Axes of the slice: x: 2, y: 2, z: 4, core: 2. Of those that a mesh axis runs over, the one named last changes fastest.
Arguments:
- acts: bfloat16 [4, 2048, 4096], P('groups', 'dp'), parts along dimension 0, may hold values from -6 to 6
- grad_query: bfloat16 [4, 2048, 8192], P('groups', 'dp', 'tensor'), parts along dimension 0, may hold values from -6 to 6
- keyvalue_gradient: bfloat16 [4, 2048, 2, 512], P('groups', 'dp', None, 'tensor'), parts along dimension 0, may hold values from -6 to 6
- attn_out: bfloat16 [4, 2048, 8192], P('groups', 'dp', 'tensor'), parts along dimension 0, may hold values from -6 to 6
- grad_out: bfloat16 [4, 2048, 4096], P('groups', 'dp'), parts along dimension 0, may hold values from -6 to 6
- seq_lengths: int32 [8, 16], P('dp', 'groups'), parts along dimension 1, may hold values from 1 to 64, 256 in all within a row
- group_ids: int32 [8, 16], P('dp', 'groups'), parts along dimension 1, may hold values from 0 to 1
- rewards: float32 [8, 16], P('dp', 'groups'), parts along dimension 1, may hold values from -8 to 8
- wide_params: float32 [4, 4096, 256], P('groups', ('dp', 'tensor')), parts along dimension 0, may hold values from -0.3 to 0.3
- wide_moments: float32 [2, 4, 4096, 256], P(None, 'groups', ('dp', 'tensor')), parts along dimension 1, may hold values from -4 to 4, as said below
- head_params: float32 [4, 64, 128, 128], P('groups', 'tensor', 'dp'), parts along dimension 0, may hold values from -0.3 to 0.3
- head_moments: float32 [2, 4, 64, 128, 128], P(None, 'groups', 'tensor', 'dp'), parts along dimension 1, may hold values from -4 to 4, as said below
- key_value_adapters: float32 [4, 4, 128, 128], P('groups', 'tensor', 'dp'), parts along dimension 0, may hold values from -0.3 to 0.3
- kv_moments: float32 [2, 4, 4, 128, 128], P(None, 'groups', 'tensor', 'dp'), parts along dimension 1, may hold values from -4 to 4, as said below
- base_query: bfloat16 [2, 64, 128, 4096], P(None, 'tensor', None, 'dp'), may hold values from -0.1796875 to 0.1796875
- frozen_key_rows: bfloat16 [2, 4, 128, 4096], P(None, 'tensor', None, 'dp'), may hold values from -0.1796875 to 0.1796875
- rotary_rows: int32 [128], replicated, may hold values from 0 to 127, each once
- rollout_group_order: int32 [4], replicated, may hold values from 0 to 3, each once
Outputs:
- new_wide: float32 [4, 4096, 256], P('groups', ('dp', 'tensor')), parts along dimension 0
- new_wide_moments: float32 [2, 4, 4096, 256], P(None, 'groups', ('dp', 'tensor')), parts along dimension 1
- new_head: float32 [4, 64, 128, 128], P('groups', 'tensor', 'dp'), parts along dimension 0
- new_head_moments: float32 [2, 4, 64, 128, 128], P(None, 'groups', 'tensor', 'dp'), parts along dimension 1
- new_kv: float32 [4, 4, 128, 128], P('groups', 'tensor', 'dp'), parts along dimension 0
- new_kv_moments: float32 [2, 4, 4, 128, 128], P(None, 'groups', 'tensor', 'dp'), parts along dimension 1
- merged_query: bfloat16 [4, 64, 128, 4096], P('groups', 'tensor', None, 'dp'), parts along dimension 0
- merged_key: bfloat16 [4, 4, 128, 4096], P('groups', 'tensor', None, 'dp'), parts along dimension 0
There are 2 independent parts, one for each index of `groups`. A program takes and returns all parts, laid end to end along the dimension named above; an argument that names none is the same for every part. Nothing has to cross between parts.
Inputs may be any that keep to these rules, and one draw needn't show every extreme that they name: `seq_lengths`: each row sums to 256, and one sequence of every row has exactly 64 tokens. `rotary_rows`: a permutation. `rollout_group_order`: a permutation. `wide_moments`: entry 0 holds first moments, entry 1 positive second moments. `head_moments`: entry 0 holds first moments, entry 1 positive second moments. `kv_moments`: entry 0 holds first moments, entry 1 positive second moments.
All inputs are finite; a program needn't handle non-finite values.
Results may differ from a plain program's by a relative error of at most 0.0059.
Values may be sent and summed in bfloat16 or wider, within the bound.
A program may use at most 192 MiB of HBM per device.

v0:
```python
import jax
import jax.numpy as jnp
from jax import lax
from jax.sharding import PartitionSpec as P

adapter_scale = 2.0
beta_one = 0.9
beta_two = 0.99
learn_rate = 0.002
decay_rate = 0.01
adam_eps = 1e-08
bias_one = 1.0 - beta_one**20
bias_two = 1.0 - beta_two**20


def token_weights(seq_lengths, group_ids, rewards, count):
    seq_ends = jnp.cumsum(seq_lengths, axis=-1)
    starts = seq_ends - seq_lengths
    places = jnp.arange(count, dtype=jnp.int32)
    member = (
        (places[None, :, None] >= starts[:, None, :])
        & (places[None, :, None] < seq_ends[:, None, :])
    ).astype(jnp.float32)
    same_group = (group_ids[:, :, None] == group_ids[:, None, :]).astype(jnp.float32)
    group_mean = jnp.sum(same_group * rewards[:, None, :], axis=-1) / jnp.sum(same_group, axis=-1)
    advantage = rewards - group_mean
    per_seq = advantage / seq_lengths.astype(jnp.float32)
    return jnp.sum(member * per_seq[:, None, :], axis=-1).reshape(-1)


def contracted_rows(left, right):
    return lax.dot_general(
        left, right, (((0,), (0,)), ((), ())), preferred_element_type=jnp.float32
    )


def adamw(parameter, moments, gradient):
    first_moment = beta_one * moments[0] + (1.0 - beta_one) * gradient
    second_moment = beta_two * moments[1] + (1.0 - beta_two) * gradient * gradient
    update = first_moment / bias_one / (jnp.sqrt(second_moment / bias_two) + adam_eps)
    return (
        parameter - learn_rate * (update + decay_rate * parameter),
        jnp.stack([first_moment, second_moment]),
    )


def merge_local(base_rows, rank_up, rank_down, row_order, head_index):
    selected_frozen = jnp.take(jnp.take(base_rows, head_index, axis=1), row_order, axis=2)
    picked_up = jnp.take(jnp.take(rank_up, head_index, axis=1), row_order, axis=2)
    low_rank_product = jnp.einsum(
        "lhjr,ldr->lhjd", picked_up, rank_down, preferred_element_type=jnp.float32
    )
    return (selected_frozen.astype(jnp.float32) + adapter_scale * low_rank_product).astype(
        jnp.bfloat16
    )


def body(
    acts,
    grad_query,
    keyvalue_gradient,
    attn_out,
    grad_out,
    seq_lengths,
    group_ids,
    rewards,
    wide_params,
    wide_moments,
    head_params,
    head_moments,
    key_value_adapters,
    kv_moments,
    base_query,
    frozen_key_rows,
    rotary_rows,
    rollout_group_order,
):
    tensor_size = lax.axis_size("tensor")
    tensor_pos = lax.axis_index("tensor")
    layers, tokens, model_width = acts.shape
    adapter_rank_size = wide_params.shape[2] // 4
    weight_col = token_weights(seq_lengths, group_ids, rewards, tokens)[:, None]
    work_wide = lax.all_gather(
        wide_params.astype(jnp.bfloat16), ("dp", "tensor"), axis=1, tiled=True
    )
    work_head, work_kv = (
        lax.all_gather(head_params.astype(jnp.bfloat16), "dp", axis=2, tiled=True),
        lax.all_gather(key_value_adapters.astype(jnp.bfloat16), "dp", axis=2, tiled=True),
    )
    wide_terms = []
    head_terms = []
    kv_terms = []
    for layer_num in range(layers):
        input_rows = acts[layer_num]
        query_gradient = grad_query[layer_num]
        key_gradient = keyvalue_gradient[layer_num, :, 0]
        value_gradient = keyvalue_gradient[layer_num, :, 1]
        attention_piece = attn_out[layer_num]
        output_gradient = grad_out[layer_num]
        a_in = work_wide[layer_num, :, : 3 * adapter_rank_size]
        b_out = work_wide[layer_num, :, 3 * adapter_rank_size :]
        flat_head = work_head[layer_num].reshape(-1, 2 * adapter_rank_size)
        flat_kv = work_kv[layer_num].reshape(-1, 2 * adapter_rank_size)
        hidden_weighted = (
            weight_col * jnp.dot(input_rows, a_in, preferred_element_type=jnp.float32)
        ).astype(jnp.bfloat16)
        g_part = jnp.concatenate(
            [
                jnp.dot(
                    query_gradient,
                    flat_head[:, :adapter_rank_size],
                    preferred_element_type=jnp.float32,
                ),
                jnp.dot(
                    key_gradient, flat_kv[:, :adapter_rank_size], preferred_element_type=jnp.float32
                ),
                jnp.dot(
                    value_gradient,
                    flat_kv[:, adapter_rank_size:],
                    preferred_element_type=jnp.float32,
                ),
            ],
            axis=1,
        )
        h_part = jnp.dot(
            attention_piece, flat_head[:, adapter_rank_size:], preferred_element_type=jnp.float32
        )
        g_sum, h_sum = lax.psum((g_part, h_part), "tensor")
        gate_weighted = (weight_col * g_sum).astype(jnp.bfloat16)
        hidden_output = (weight_col * h_sum).astype(jnp.bfloat16)
        gate_output = (
            weight_col * jnp.dot(output_gradient, b_out, preferred_element_type=jnp.float32)
        ).astype(jnp.bfloat16)
        wide_terms.append(
            adapter_scale
            * jnp.concatenate(
                [
                    contracted_rows(input_rows, gate_weighted),
                    contracted_rows(output_gradient, hidden_output),
                ],
                axis=1,
            )
        )
        head_terms.append(
            (
                adapter_scale
                * jnp.concatenate(
                    [
                        contracted_rows(query_gradient, hidden_weighted[:, :adapter_rank_size]),
                        contracted_rows(attention_piece, gate_output),
                    ],
                    axis=1,
                )
            ).reshape(work_head.shape[1:])
        )
        kv_terms.append(
            (
                adapter_scale
                * jnp.concatenate(
                    [
                        contracted_rows(
                            key_gradient,
                            hidden_weighted[:, adapter_rank_size : 2 * adapter_rank_size],
                        ),
                        contracted_rows(
                            value_gradient, hidden_weighted[:, 2 * adapter_rank_size :]
                        ),
                    ],
                    axis=1,
                )
            ).reshape(work_kv.shape[1:])
        )
    wide_stack = jnp.stack(wide_terms)
    wide_full = lax.psum_scatter(wide_stack, "dp", scatter_dimension=1, tiled=True)
    piece_rows = wide_full.shape[1] // tensor_size
    wide_grad = lax.dynamic_slice_in_dim(wide_full, tensor_pos * piece_rows, piece_rows, 1)
    head_grad, kv_grad = (
        lax.psum_scatter(jnp.stack(head_terms), "dp", scatter_dimension=2, tiled=True),
        lax.psum_scatter(jnp.stack(kv_terms), "dp", scatter_dimension=2, tiled=True),
    )
    new_wide, new_wide_moments = adamw(wide_params, wide_moments, wide_grad)
    new_head, new_head_moments = adamw(head_params, head_moments, head_grad)
    new_kv, new_kv_moments = adamw(key_value_adapters, kv_moments, kv_grad)
    rank_down = lax.all_gather(
        new_wide[..., : 2 * adapter_rank_size].astype(jnp.bfloat16), "tensor", axis=1, tiled=True
    )
    rank_query, rank_key = (
        lax.all_gather(
            new_head[..., :adapter_rank_size].astype(jnp.bfloat16), "dp", axis=2, tiled=True
        ),
        lax.all_gather(
            new_kv[..., :adapter_rank_size].astype(jnp.bfloat16), "dp", axis=2, tiled=True
        ),
    )
    local_groups = rank_key.shape[1]
    group_width = rank_query.shape[1] // local_groups
    group_slots = tensor_pos * local_groups + jnp.arange(local_groups, dtype=jnp.int32)
    source_groups = jnp.take(rollout_group_order, group_slots)
    query_heads = (
        source_groups[:, None] * group_width + jnp.arange(group_width, dtype=jnp.int32)[None, :]
    ).reshape(-1)
    local_query = merge_local(
        base_query,
        rank_query,
        rank_down[..., :adapter_rank_size],
        rotary_rows,
        jnp.arange(rank_query.shape[1], dtype=jnp.int32),
    )
    local_key = merge_local(
        frozen_key_rows,
        rank_key,
        rank_down[..., adapter_rank_size:],
        rotary_rows,
        jnp.arange(local_groups, dtype=jnp.int32),
    )
    gathered_query, gathered_key = (
        lax.all_gather(local_query, "tensor", axis=1, tiled=True),
        lax.all_gather(local_key, "tensor", axis=1, tiled=True),
    )
    merged_query = jnp.take(gathered_query, query_heads, axis=1)
    merged_key = jnp.take(gathered_key, source_groups, axis=1)
    return (
        new_wide,
        new_wide_moments,
        new_head,
        new_head_moments,
        new_kv,
        new_kv_moments,
        merged_query,
        merged_key,
    )


def solution(mesh):
    placed = (
        P("groups", "dp", None),
        P("groups", "dp", "tensor"),
        P("groups", "dp", None, "tensor"),
        P("groups", "dp", "tensor"),
        P("groups", "dp", None),
        P("dp", "groups"),
        P("dp", "groups"),
        P("dp", "groups"),
        P("groups", ("dp", "tensor"), None),
        P(None, "groups", ("dp", "tensor"), None),
        P("groups", "tensor", "dp", None),
        P(None, "groups", "tensor", "dp", None),
        P("groups", "tensor", "dp", None),
        P(None, "groups", "tensor", "dp", None),
        P(None, "tensor", None, "dp"),
        P(None, "tensor", None, "dp"),
        P(),
        P(),
    )
    return jax.shard_map(
        body,
        mesh=mesh,
        in_specs=placed,
        out_specs=(
            P("groups", ("dp", "tensor"), None),
            P(None, "groups", ("dp", "tensor"), None),
            P("groups", "tensor", "dp", None),
            P(None, "groups", "tensor", "dp", None),
            P("groups", "tensor", "dp", None),
            P(None, "groups", "tensor", "dp", None),
            P("groups", "tensor", None, "dp"),
            P("groups", "tensor", None, "dp"),
        ),
        check_vma=False,
    )
```

profile of v0, /device:TPU:0, one launch (start us, length us, event | category | flops | bytes accessed | tf_op | source)
XLA Modules:
  0.0 623.0 jit_solution(11279884756734092890)
XLA Ops:
  12.6 32.6 %all_gather.25 = bf16[2,2,128,128]{3,2,1,0:T(8,128)(2,1)S(1)} all-gather(bf16[2,2,16,128]{3,2,1,0:T(8,128)(2,1)S(1)} %convert_element_type.66), channel_id=1, replica_groups=mesh['groups'=2,'dp'=8,'tensor'=2] {'dp'}, dimensions={2}, use_global_device_ids=true | all-gather | bytes 147456 | tf_op jit(solution)/shard_map/all_gather | solution.py:88
  51.4 13.4 %all-gather.6.cloned.1.call-done = bf16[2,32,128,128]{3,2,1,0:T(8,128)(2,1)} async-done(((bf16[2,32,16,128]{3,2,1,0:T(8,128)(2,1)}), bf16[2,32,128,128]{3,2,1,0:T(8,128)(2,1)}) %all-gather.6.cloned.1.call-update) | async-done | bytes 2097168 | tf_op jit(solution)/shard_map/all_gather | solution.py:87
  74.2 42.4 %all-gather.8.cloned.1.call-done = bf16[2,4096,256]{2,1,0:T(8,128)(2,1)} async-done(((bf16[2,256,256]{2,1,0:T(8,128)(2,1)}), bf16[2,4096,256]{2,1,0:T(8,128)(2,1)}) %all-gather.8.cloned.1.call-update) | async-done | bytes 4194320 | tf_op jit(solution)/shard_map/all_gather | solution.py:83
  116.6 3.4 fusion.69
  122.1 4.4 fusion.49
  126.6 5.3 fusion.55
  131.9 3.5 fusion.66
  138.1 3.0 copy.168
  143.6 4.0 copy.167
  150.0 4.1 copy.170
  156.4 4.1 copy.169
  160.5 4.4 maximum_multiply_fusion.2
  171.7 4.3 convolution_bitcast_fusion
  186.8 67.1 %reduce-scatter.5.cloned.1.call-done = f32[2,32,16,128]{3,1,0,2:T(8,128)} async-done(((f32[2,32,128,128]{3,1,0,2:T(8,128)}), f32[2,32,16,128]{3,1,0,2:T(8,128)}) %reduce-scatter.5.cloned.1.call-update) | async-done | bytes 524304 | tf_op jit(solution)/shard_map/reduce_scatter | solution.py:178
  253.9 2.9 fusion.97
  262.5 3.9 pad_maximum_fusion
  270.6 8.5 %gather_fusion.1 = bf16[32,2,128,512]{3,2,1,0:T(8,128)(2,1)} fusion(bf16[2,32,128,512]{3,2,1,0:T(8,128)(2,1)} %param.32, s32[1024]{0:T(1024)S(1)} %pad_clamp_fusion.4), kind=kCustom, calls=%fused_computation.1 | custom fusion | bytes 16777344 | tf_op jit(solution)/shard_map/jit(_take)/gather | solution.py:48
  279.1 7.5 %select_bitcast_fusion.1 = bf16[2,32,128,512]{3,2,0,1:T(8,128)(2,1)} fusion(bf16[32,2,128,512]{3,2,1,0:T(8,128)(2,1)} %gather_fusion.1, pred[32]{0:T(512)(128)(4,1)S(1)} %iota_compare_fusion.3), kind=kLoop, calls=%fused_computation.16 | loop fusion | flops 4194304 | bytes 16777248 | tf_op jit(solution)/shard_map/jit(_take)/select_n | solution.py:48
  286.7 11.4 %copy.186 = bf16[2,32,128,512]{3,1,2,0:T(8,128)(2,1)} copy(bf16[2,32,128,512]{3,2,0,1:T(8,128)(2,1)} %select_bitcast_fusion.1) | data formatting | bytes 16777216 | tf_op jit(solution)/shard_map/jit(_take)/select_n | solution.py:48
  299.5 10.1 %gather_fusion.2 = bf16[128,2,32,512]{3,2,1,0:T(8,128)(2,1)} fusion(bf16[2,32,128,512]{3,1,2,0:T(8,128)(2,1)} %copy.186, s32[1024]{0:T(1024)S(1)} %pad_clamp_fusion.3), kind=kCustom, calls=%fused_computation.2 | custom fusion | bytes 16777728 | tf_op jit(solution)/shard_map/jit(_take)/gather | solution.py:48
  313.3 14.8 %all-reduce.5.cloned.1.call-done = f32[2,2,128,128]{3,1,0,2:T(2,128)} async-done(((f32[2,2,128,128]{3,1,0,2:T(2,128)}), f32[2,2,128,128]{3,1,0,2:T(2,128)}) %all-reduce.5.cloned.1.call-update) | async-done | bytes 262160
  328.9 30.8 %all_gather.30 = bf16[2,2,128,64]{3,1,0,2:T(2,128)(2,1)S(1)} all-gather(bf16[2,2,16,64]{3,1,0,2:T(2,128)(2,1)S(1)} %slice.383), channel_id=1, replica_groups=mesh['groups'=2,'dp'=8,'tensor'=2] {'dp'}, dimensions={2}, use_global_device_ids=true | all-gather | bytes 73728 | tf_op jit(solution)/shard_map/all_gather | solution.py:191
  361.8 17.6 %all-gather.10.cloned.1.call-done = bf16[2,32,128,64]{3,1,0,2:T(8,128)(2,1)} async-done(((bf16[2,32,16,64]{3,1,0,2:T(8,128)(2,1)}), bf16[2,32,128,64]{3,1,0,2:T(8,128)(2,1)}) %all-gather.10.cloned.1.call-update) | async-done | bytes 1048592 | tf_op jit(solution)/shard_map/all_gather | solution.py:188
  379.4 3.3 copy.188
  384.6 3.9 copy.189
  390.7 3.3 select_bitcast_fusion.2
  394.0 138.1 %reduce-scatter.3.cloned.1.call-done = f32[2,512,256]{1,2,0:T(8,128)} async-done(((f32[2,4096,256]{1,2,0:T(8,128)}), f32[2,512,256]{1,2,0:T(8,128)}) %reduce-scatter.3.cloned.1.call-update) | async-done | bytes 1048592 | tf_op jit(solution)/shard_map/reduce_scatter | solution.py:174
  537.6 23.0 %fusion = bf16[2,32,128,512]{3,2,1,0:T(8,128)(2,1)} fusion(bf16[128,2,32,512]{3,2,1,0:T(8,128)(2,1)} %gather_fusion.2, pred[128]{0:T(512)(128)(4,1)S(1)} %compare_and_fusion.1, bf16[2,32,128,64]{3,1,0,2:T(8,128)(2,1)} %select_bitcast_fusion.2, bf16[2,512,128]{1,2,0:T(8,128)(2,1)S(1)} %all_gather.28), kind=kOutput, calls=%fused_computation.12 | convolution fusion | flops 557842432 | bytes 17957376 | tf_op jit(solution)/shard_map/lhjr,ldr->lhjd/dot_general | solution.py:50
  573.0 16.9 %all-gather.12.cloned.1.call-done = bf16[2,64,128,512]{3,2,1,0:T(8,128)(2,1)} async-done(((bf16[2,32,128,512]{3,2,1,0:T(8,128)(2,1)}), bf16[2,64,128,512]{3,2,1,0:T(8,128)(2,1)}) %all-gather.12.cloned.1.call-update) | async-done | bytes 16777232 | tf_op jit(solution)/shard_map/all_gather | solution.py:217
  589.9 11.0 %gather_fusion.5 = bf16[32,2,128,512]{3,2,1,0:T(8,128)(2,1)} fusion(bf16[2,64,128,512]{3,2,1,0:T(8,128)(2,1)} %all-gather.12.cloned.1.call-done, s32[1024]{0:T(1024)S(1)} %pad_clamp_fusion.2), kind=kCustom, calls=%fused_computation.5 | custom fusion | bytes 16777344 | tf_op jit(solution)/shard_map/jit(_take)/gather | solution.py:220
  600.9 7.5 %select_bitcast_fusion = bf16[2,32,128,512]{3,2,0,1:T(8,128)(2,1)} fusion(bf16[32,2,128,512]{3,2,1,0:T(8,128)(2,1)} %gather_fusion.5, pred[32]{0:T(512)(128)(4,1)S(1)} %compare_and_fusion.2), kind=kLoop, calls=%fused_computation.15 | loop fusion | flops 4194304 | bytes 16777248 | tf_op jit(solution)/shard_map/jit(_take)/select_n | solution.py:220
  608.4 7.8 %copy.200 = bf16[2,32,128,512]{3,2,1,0:T(8,128)(2,1)} copy(bf16[2,32,128,512]{3,2,0,1:T(8,128)(2,1)} %select_bitcast_fusion) | data formatting | bytes 16777216
  (189 shorter events, 89.2 us)
Async XLA Ops:
  7.2 291.0 %copy-start = (bf16[2,2,128,512]{3,2,1,0:T(8,128)(2,1)S(1)}, bf16[2,2,128,512]{3,2,1,0:T(8,128)(2,1)}, u32[]{:S(2)}) copy-start(bf16[2,2,128,512]{3,2,1,0:T(8,128)(2,1)} %param.33) | copy-start | bytes 1572868
  7.2 57.7 %all-gather.6.cloned.1.call-start = ((), (), s32[]{:S(2)}) async-start(), calls=%async_computation.2 | async-start | bytes 2359296 | tf_op jit(solution)/shard_map/all_gather | solution.py:87
  9.1 107.5 %all-gather.8.cloned.1.call-start = ((), (), s32[]{:S(2)}) async-start(), calls=%async_computation.4 | async-start | bytes 4456448 | tf_op jit(solution)/shard_map/all_gather | solution.py:83
  10.9 158.5 %all-reduce.7.cloned.1.call-start = ((), (), s32[]{:S(2)}) async-start(), calls=%async_computation.10 | async-start | bytes 1048576 | tf_op jit(solution)/shard_map/psum | solution.py:128
  64.8 2.8 copy-start.5
  66.7 3.3 copy-start.8
  74.0 180.0 %reduce-scatter.5.cloned.1.call-start = ((), (), s32[]{:S(2)}) async-start(), calls=%async_computation.5 | async-start | bytes 4718592 | tf_op jit(solution)/shard_map/reduce_scatter | solution.py:178
  116.6 4.0 copy-start.6
  131.9 3.7 copy-start.7
  135.5 2.6 copy-start.24
  167.4 160.7 %all-reduce.5.cloned.1.call-start = ((), (), s32[]{:S(2)}) async-start(), calls=%async_computation.9 | async-start | bytes 524288
  169.5 6.6 %copy-start.9 = (bf16[2,256,4096]{2,1,0:T(8,128)(2,1)S(1)}, bf16[2,256,4096]{2,1,0:T(8,128)(2,1)}, u32[]{:S(2)}) copy-start(bf16[2,256,4096]{2,1,0:T(8,128)(2,1)} %param.18) | copy-start | bytes 12582916
  169.5 6.6 %copy-start.22 = (f32[256,192]{0,1:T(8,128)S(1)}, f32[256,192]{0,1:T(8,128)}, u32[]{:S(2)}) copy-start(f32[256,192]{0,1:T(8,128)} %get-tuple-element.53) | copy-start | bytes 589828
  171.7 6.6 %copy-start.20 = (bf16[1,256,1,256]{3,2,1,0:T(2,128)(2,1)S(1)}, bf16[1,256,1,256]{3,2,1,0:T(2,128)(2,1)}, u32[]{:S(2)}) copy-start(bf16[1,256,1,256]{3,2,1,0:T(2,128)(2,1)} %copy-done.19) | copy-start | bytes 393220
  176.1 77.9 %copy-start.10 = (f32[2,32,16,128]{3,2,1,0:T(8,128)S(1)}, f32[2,32,16,128]{3,2,1,0:T(8,128)}, u32[]{:S(2)}) copy-start(f32[2,32,16,128]{3,2,1,0:T(8,128)} %param.28) | copy-start | bytes 1572868
  185.9 71.7 %copy-start.26 = (f32[256,64]{0,1:T(8,128)S(1)}, f32[256,64]{0,1:T(8,128)}, u32[]{:S(2)}) copy-start(f32[256,64]{0,1:T(8,128)} %get-tuple-element.52) | copy-start | bytes 196612
  186.8 192.7 %all-gather.10.cloned.1.call-start = ((), (), s32[]{:S(2)}) async-start(), calls=%async_computation.6 | async-start | bytes 2359296 | tf_op jit(solution)/shard_map/all_gather | solution.py:188
  257.6 274.5 %reduce-scatter.3.cloned.1.call-start = ((), (), s32[]{:S(2)}) async-start(), calls=%async_computation.3 | async-start | bytes 9437184 | tf_op jit(solution)/shard_map/reduce_scatter | solution.py:174
  257.6 2.5 copy-start.3
  266.5 303.3 %all-gather.14.cloned.1.call-start = ((), (), s32[]{:S(2)}) async-start(), calls=%async_computation.8 | async-start | bytes 1572864 | tf_op jit(solution)/shard_map/all_gather | solution.py:218
  286.7 12.7 %copy-start.28 = (s32[128]{0:T(128)S(1)}, s32[128]{0:T(128)}, u32[]{:S(2)}) copy-start(s32[128]{0:T(128)} %param.34) | copy-start | bytes 1540
  299.4 12.5 %copy-start.29 = (u32[32]{0:T(128)S(1)}, u32[32]{0:T(128)}, u32[]{:S(2)}) copy-start(u32[32]{0:T(128)} %constant.216) | copy-start | bytes 388
  299.4 13.8 %copy-start.27 = (f32[2,2,2,16,128]{4,3,2,1,0:T(8,128)S(1)}, f32[2,2,2,16,128]{4,3,2,1,0:T(8,128)}, u32[]{:S(2)}) copy-start(f32[2,2,2,16,128]{4,3,2,1,0:T(8,128)} %param.31) | copy-start | bytes 196612
  299.5 28.6 %copy-start.23 = (f32[2,2,16,128]{3,2,1,0:T(8,128)S(1)}, f32[2,2,16,128]{3,2,1,0:T(8,128)}, u32[]{:S(2)}) copy-start(f32[2,2,16,128]{3,2,1,0:T(8,128)} %param.30) | copy-start | bytes 98308
  388.6 143.6 %copy-start.14 = (f32[2,256,256]{1,2,0:T(8,128)S(1)}, f32[2,256,256]{1,2,0:T(8,128)}, u32[]{:S(2)}) copy-start(f32[2,256,256]{1,2,0:T(8,128)} %copy.165) | copy-start | bytes 1572868
  390.7 141.4 %copy-start.15 = (f32[1,2,256,256]{2,3,1,0:T(8,128)S(1)}, f32[1,2,256,256]{2,3,1,0:T(8,128)}, u32[]{:S(2)}) copy-start(f32[1,2,256,256]{2,3,1,0:T(8,128)} %copy.204) | copy-start | bytes 1572868
  390.7 141.4 %copy-start.16 = (f32[1,2,256,256]{2,3,1,0:T(8,128)S(1)}, f32[1,2,256,256]{2,3,1,0:T(8,128)}, u32[]{:S(2)}) copy-start(f32[1,2,256,256]{2,3,1,0:T(8,128)} %copy.209) | copy-start | bytes 1572868
  532.1 4.3 copy-start.21
  537.6 52.3 %all-gather.12.cloned.1.call-start = ((), (), s32[]{:S(2)}) async-start(), calls=%async_computation.7 | async-start | bytes 25165824 | tf_op jit(solution)/shard_map/all_gather | solution.py:217
  560.6 4.0 copy-start.12
  560.6 4.3 copy-start.11
  608.4 7.8 %copy-start.1 = (bf16[2,2,128,512]{3,2,1,0:T(8,128)(2,1)S(1)}, bf16[2,2,128,512]{3,2,1,0:T(8,128)(2,1)}, u32[]{:S(2)}) copy-start(bf16[2,2,128,512]{3,2,1,0:T(8,128)(2,1)} %param.33) | copy-start | bytes 1572868
  (7 other events, 8.2 us)
Sparse Core Ops, SparseCore 0:
  10.6 54.1 all-gather.5
  67.6 48.9 all-gather.7
  119.7 17.3 all-reduce.6
  167.5 86.3 reduce-scatter.4
  257.7 70.3 all-reduce.4
  330.2 49.1 all-gather.9
  384.1 148.0 reduce-scatter.2
  537.7 8.0 all-gather.13
  560.8 29.0 all-gather.11
where the time goes:
time: 629 us; the launch traced here: 623 us
  waiting for transfers between devices  311 us (49%)
  local copies, waits for them, and re-layouts  115 us (18%)
  blocking collectives  65.4 us (10%)
  matrix products  65.3 us (10%)
  other arithmetic  50.5 us (8%)
  between operations  15.2 us (2%)
    reduce_scatter x1, waiting for transfers between devices, body(): lax.psum_scatter(wide_stack, 'dp', scatter_dimension=1, tiled=True)  138 us
    reduce_scatter x1, waiting for transfers between devices, body(): lax.psum_scatter(jnp.stack(head_terms), 'dp', scatter_dimension=2, tiled=...  67.1 us
    all_gather x1, waiting for transfers between devices, body(): lax.all_gather(wide_params.astype(jnp.bfloat16), ('dp', 'tensor'), axis=1...  42.4 us
    all_gather x1, blocking collectives, body(): lax.all_gather(key_value_adapters.astype(jnp.bfloat16), 'dp', axis=2, til...  32.6 us
    unnamed x74, local copies, waits for them, and re-layouts  31.5 us
    all_gather x1, blocking collectives, body(): lax.all_gather(new_kv[..., :adapter_rank_size].astype(jnp.bfloat16), 'dp'...  30.8 us
    dot_general x12, matrix products, contracted_rows(): lax.dot_general(left, right, (((0,), (0,)), ((), ())), preferred_element_...  28 us
    dot_general x2, matrix products, merge_local(): jnp.einsum('lhjr,ldr->lhjd', picked_up, rank_down, preferred_element_type...  24.1 us
  transfers between devices with their start and end apart: 9, of which 7 were waited for; matrix products, arithmetic and copies ran while one was open for 31% of the time, Pallas kernels for 0%

commit v1 on v0

v1 whole, which is shorter than its diff:
```python
import functools

import jax
import jax.numpy as jnp
from jax import lax
from jax.experimental import pallas as pl
from jax.experimental.pallas import tpu as pltpu
from jax.sharding import PartitionSpec as P

adapter_scale = 2.0
beta_one = 0.9
beta_two = 0.99
learn_rate = 0.002
decay_rate = 0.01
adam_eps = 1e-08
bias_one = 1.0 - beta_one**20
bias_two = 1.0 - beta_two**20


def token_weights(seq_lengths, group_ids, rewards, count):
    seq_ends = jnp.cumsum(seq_lengths, axis=-1)
    starts = seq_ends - seq_lengths
    places = jnp.arange(count, dtype=jnp.int32)
    member = (
        (places[None, :, None] >= starts[:, None, :])
        & (places[None, :, None] < seq_ends[:, None, :])
    ).astype(jnp.float32)
    same_group = (group_ids[:, :, None] == group_ids[:, None, :]).astype(jnp.float32)
    group_mean = jnp.sum(same_group * rewards[:, None, :], axis=-1) / jnp.sum(same_group, axis=-1)
    advantage = rewards - group_mean
    per_seq = advantage / seq_lengths.astype(jnp.float32)
    return jnp.sum(member * per_seq[:, None, :], axis=-1).reshape(-1)


def contracted_rows(left, right):
    return lax.dot_general(
        left, right, (((0,), (0,)), ((), ())), preferred_element_type=jnp.float32
    )


def adamw(parameter, moments, gradient):
    first_moment = beta_one * moments[0] + (1.0 - beta_one) * gradient
    second_moment = beta_two * moments[1] + (1.0 - beta_two) * gradient * gradient
    update = first_moment / bias_one / (jnp.sqrt(second_moment / bias_two) + adam_eps)
    return (
        parameter - learn_rate * (update + decay_rate * parameter),
        jnp.stack([first_moment, second_moment]),
    )


MESH = pl.DeviceIdType.MESH
ROW_STEP = 32


def remote(src, dst, send_sem, recv_sem, device):
    return pltpu.make_async_remote_copy(
        src_ref=src,
        dst_ref=dst,
        send_sem=send_sem,
        recv_sem=recv_sem,
        device_id=device,
        device_id_type=MESH,
    )


def place(count):
    me = lax.axis_index("dp")
    return me, me // 2, me % 2, count // 2


def greet(z, m, partners):
    me = lax.axis_index("dp")
    barrier = pltpu.get_barrier_semaphore()
    for device in partners:
        pl.semaphore_signal(barrier, inc=1, device_id=device, device_id_type=MESH)

    @pl.when(z > 0)
    def _():
        pl.semaphore_signal(barrier, inc=1, device_id={"dp": me - 2}, device_id_type=MESH)

    @pl.when(z < m - 1)
    def _():
        pl.semaphore_signal(barrier, inc=1, device_id={"dp": me + 2}, device_id_type=MESH)

    ends = jnp.where(z > 0, 1, 0) + jnp.where(z < m - 1, 1, 0)
    pl.semaphore_wait(barrier, len(partners) + ends)


def gather_kernel(count, pieces, share, swaps, *refs):
    refs = list(refs)
    take = lambda k: [refs.pop(0) for _ in range(k)]
    ins, swap_ins = take(pieces), take(swaps)
    outs, others, swap_outs = take(pieces), take(pieces if share else 0), take(swaps)
    send_right, send_left, send_row, recv, local_sem = take(5)
    send_core, recv_core = take(2) if share else (None, None)
    send_swap, recv_swap = take(2) if swaps else (None, None)
    me, z, y, m = place(count)
    row_mate = {"dp": me + 1 - 2 * y}
    core_mate = {"tensor": 1 - lax.axis_index("tensor")}
    has_left, has_right = z > 0, z < m - 1
    greet(z, m, [row_mate] + ([core_mate] if share or swaps else []))

    def right(p, src, k):
        slot = (z - k) * 2 + y
        return remote(src(slot), outs[p].at[slot], send_right.at[p, k], recv.at[p, slot], {"dp": me + 2})

    def left(p, src, k):
        slot = (z + k) * 2 + y
        return remote(src(slot), outs[p].at[slot], send_left.at[p, k], recv.at[p, slot], {"dp": me - 2})

    def across(p, src, zz):
        slot = zz * 2 + y
        return remote(src(slot), outs[p].at[slot], send_row.at[p, zz], recv.at[p, slot], row_mate)

    def to_core(p, src, slot):
        return remote(src(slot), others[p].at[slot], send_core.at[p, slot], recv_core.at[p, slot], core_mate)

    def arrive(p, slot):
        remote(outs[p].at[slot], outs[p].at[slot], send_row.at[p, 0], recv.at[p, slot], row_mate).wait_recv()

    own = [lambda slot, r=r: r for r in ins]
    held = [lambda slot, r=r: r.at[slot] for r in outs]

    for s in range(swaps):
        remote(swap_ins[s], swap_outs[s], send_swap.at[s], recv_swap.at[s], core_mate).start()
    for p in range(pieces):

        @pl.when(has_right)
        def _():
            right(p, own[p], 0).start()

        @pl.when(has_left)
        def _():
            left(p, own[p], 0).start()

        across(p, own[p], z).start()
        if share:
            to_core(p, own[p], me).start()
        pltpu.make_async_copy(ins[p], outs[p].at[me], local_sem.at[p]).start()

    for k in range(1, m):
        for p in range(pieces):

            @pl.when(z - k >= 0)
            def _():
                slot = (z - k) * 2 + y
                arrive(p, slot)

                @pl.when(has_right)
                def _():
                    right(p, held[p], k).start()

                across(p, held[p], z - k).start()
                if share:
                    to_core(p, held[p], slot).start()

            @pl.when(z + k < m)
            def _():
                slot = (z + k) * 2 + y
                arrive(p, slot)

                @pl.when(has_left)
                def _():
                    left(p, held[p], k).start()

                across(p, held[p], z + k).start()
                if share:
                    to_core(p, held[p], slot).start()

    far = 1 - y
    for zz in range(m):
        for p in range(pieces):
            slot = zz * 2 + far
            arrive(p, slot)
            if share:
                to_core(p, held[p], slot).start()
    for p in range(pieces):
        pltpu.make_async_copy(ins[p], outs[p].at[me], local_sem.at[p]).wait()
        for zz in range(m):
            across(p, held[p], zz).wait_send()
        for k in range(m):

            @pl.when(has_right & (z - k >= 0))
            def _():
                right(p, held[p], k).wait_send()

            @pl.when(has_left & (z + k < m))
            def _():
                left(p, held[p], k).wait_send()

        if share:
            for slot in range(count):
                to_core(p, held[p], slot).wait()
    for s in range(swaps):
        remote(swap_ins[s], swap_outs[s], send_swap.at[s], recv_swap.at[s], core_mate).wait()


def gather_dp(arrays, swapped, count, share, collective_id):
    pieces, swaps, m = len(arrays), len(swapped), count // 2
    stacked = [jax.ShapeDtypeStruct((count,) + a.shape, a.dtype) for a in arrays]
    dma = pltpu.SemaphoreType.DMA
    scratch = [dma((pieces, m)), dma((pieces, m)), dma((pieces, m)), dma((pieces, count)), dma((pieces,))]
    if share:
        scratch += [dma((pieces, count)), dma((pieces, count))]
    if swaps:
        scratch += [dma((swaps,)), dma((swaps,))]
    shapes = stacked + (stacked if share else []) + [
        jax.ShapeDtypeStruct(a.shape, a.dtype) for a in swapped
    ]
    anywhere = pl.BlockSpec(memory_space=pl.ANY)
    return pl.pallas_call(
        functools.partial(gather_kernel, count, pieces, share, swaps),
        out_shape=shapes,
        in_specs=[anywhere] * (pieces + swaps),
        out_specs=[anywhere] * len(shapes),
        scratch_shapes=scratch,
        compiler_params=pltpu.CompilerParams(collective_id=collective_id, has_side_effects=True),
        name="gather_pieces",
    )(*arrays, *swapped)


def add_rows(dst, terms):
    def step(i, carry):
        rows = pl.ds(pl.multiple_of(i * ROW_STEP, ROW_STEP), ROW_STEP)
        total = terms[0][rows, :].astype(jnp.float32)
        for term in terms[1:]:
            total = total + term[rows, :].astype(jnp.float32)
        dst[rows, :] = total.astype(dst.dtype)
        return carry

    lax.fori_loop(0, dst.shape[0] // ROW_STEP, step, 0)


def scatter_kernel(count, pieces, *refs):
    refs = list(refs)
    take = lambda k: [refs.pop(0) for _ in range(k)]
    ins, outs = take(pieces), take(pieces)
    from_row, from_left, from_right, leaving = take(pieces), take(pieces), take(pieces), take(pieces)
    row_send, row_recv, line_send, left_recv, right_recv = take(5)
    me, z, y, m = place(count)
    row_mate = {"dp": me + 1 - 2 * y}
    has_left, has_right = z > 0, z < m - 1
    greet(z, m, [row_mate])

    def across(p, zz):
        return remote(
            ins[p].at[zz * 2 + 1 - y], from_row[p].at[zz], row_send.at[p, zz], row_recv.at[p, zz], row_mate
        )

    def right(p, zz):
        return remote(
            leaving[p].at[zz], from_left[p].at[zz], line_send.at[p, zz], left_recv.at[p, zz], {"dp": me + 2}
        )

    def left(p, zz):
        return remote(
            leaving[p].at[zz], from_right[p].at[zz], line_send.at[p, zz], right_recv.at[p, zz], {"dp": me - 2}
        )

    for k in range(m - 1, 0, -1):
        for p in range(pieces):

            @pl.when(z + k < m)
            def _():
                across(p, z + k).start()

            @pl.when(z - k >= 0)
            def _():
                across(p, z - k).start()

    for p in range(pieces):
        across(p, z).start()

    for k in range(m - 1, 0, -1):
        for p in range(pieces):

            @pl.when(z + k < m)
            def _():
                zz = z + k
                across(p, zz).wait_recv()
                near = [ins[p].at[zz * 2 + y], from_row[p].at[zz]]

                @pl.when(has_left)
                def _():
                    right(p, zz).wait_recv()
                    add_rows(leaving[p].at[zz], near + [from_left[p].at[zz]])

                @pl.when(jnp.logical_not(has_left))
                def _():
                    add_rows(leaving[p].at[zz], near)

                right(p, zz).start()

            @pl.when(z - k >= 0)
            def _():
                zz = z - k
                across(p, zz).wait_recv()
                near = [ins[p].at[zz * 2 + y], from_row[p].at[zz]]

                @pl.when(has_right)
                def _():
                    left(p, zz).wait_recv()
                    add_rows(leaving[p].at[zz], near + [from_right[p].at[zz]])

                @pl.when(jnp.logical_not(has_right))
                def _():
                    add_rows(leaving[p].at[zz], near)

                left(p, zz).start()

    for p in range(pieces):
        across(p, z).wait_recv()
        add_rows(outs[p], [ins[p].at[me], from_row[p].at[z]])

        @pl.when(has_left)
        def _():
            right(p, z).wait_recv()
            add_rows(outs[p], [outs[p], from_left[p].at[z]])

        @pl.when(has_right)
        def _():
            left(p, z).wait_recv()
            add_rows(outs[p], [outs[p], from_right[p].at[z]])

        for zz in range(m):
            across(p, zz).wait_send()

            @pl.when(z < zz)
            def _():
                right(p, zz).wait_send()

            @pl.when(z > zz)
            def _():
                left(p, zz).wait_send()


def scatter_dp(arrays, count, collective_id):
    pieces, m = len(arrays), count // 2
    dma = pltpu.SemaphoreType.DMA
    slots = [pltpu.VMEM((m,) + a.shape[1:], a.dtype) for a in arrays]
    vmem = pl.BlockSpec(memory_space=pltpu.VMEM)
    return pl.pallas_call(
        functools.partial(scatter_kernel, count, pieces),
        out_shape=[jax.ShapeDtypeStruct(a.shape[1:], jnp.float32) for a in arrays],
        in_specs=[vmem] * pieces,
        out_specs=[vmem] * pieces,
        scratch_shapes=slots * 4 + [dma((pieces, m))] * 5,
        compiler_params=pltpu.CompilerParams(
            collective_id=collective_id, has_side_effects=True, vmem_limit_bytes=40 * 2**20
        ),
        name="sum_to_owners",
    )(*arrays)


def merge_kernel(first, heads, away_ref, near_ref, mix, here, there, up, down, out):
    away = away_ref[pl.program_id(1)]
    rank = up.shape[-1]
    down_part = down[0][:, first : first + rank]

    def run(base):
        def step(h, carry):
            mixed_up = jnp.dot(mix[...], up[0, h], preferred_element_type=jnp.float32)
            product = lax.dot_general(
                mixed_up.astype(jnp.bfloat16),
                down_part,
                (((1,), (1,)), ((), ())),
                preferred_element_type=jnp.float32,
            )
            rows = jnp.dot(mix[...], base[0, h], preferred_element_type=jnp.float32)
            out[0, h] = (rows + adapter_scale * product).astype(jnp.bfloat16)
            return carry

        lax.fori_loop(0, heads, step, 0, unroll=True)

    @pl.when(away == 0)
    def _():
        run(here)

    @pl.when(away != 0)
    def _():
        run(there)


def merge(base_here, base_there, rank_up, rank_down, mix, away, near, first):
    layers, head_count, size, width = base_here.shape
    slots = away.shape[0]
    per_slot = head_count // slots
    heads = min(8, per_slot)
    steps = per_slot // heads
    rank = rank_up.shape[-1]

    def here_map(l, g, c, away, near):
        return jnp.where(away[g] == 0, l, 0), jnp.where(away[g] == 0, near[g] * steps + c, 0), 0, 0

    def there_map(l, g, c, away, near):
        return jnp.where(away[g] == 0, 0, l), jnp.where(away[g] == 0, 0, near[g] * steps + c), 0, 0

    def slot_map(l, g, c, away, near):
        return l, g * steps + c, 0, 0

    block = (1, heads, size, width)
    return pl.pallas_call(
        functools.partial(merge_kernel, first, heads),
        out_shape=jax.ShapeDtypeStruct(base_here.shape, base_here.dtype),
        grid_spec=pltpu.PrefetchScalarGridSpec(
            num_scalar_prefetch=2,
            grid=(layers, slots, steps),
            in_specs=[
                pl.BlockSpec((size, size), lambda l, g, c, away, near: (0, 0)),
                pl.BlockSpec(block, here_map),
                pl.BlockSpec(block, there_map),
                pl.BlockSpec((1, heads, size, rank), slot_map),
                pl.BlockSpec((1, width, rank_down.shape[-1]), lambda l, g, c, away, near: (l, 0, 0)),
            ],
            out_specs=pl.BlockSpec(block, slot_map),
        ),
        compiler_params=pltpu.CompilerParams(vmem_limit_bytes=40 * 2**20),
        name="merged_rows",
    )(away, near, mix, base_here, base_there, rank_up, rank_down)


def swap_core(value):
    return lax.ppermute(value, "tensor", [(0, 1), (1, 0)])


def body(
    acts,
    grad_query,
    keyvalue_gradient,
    attn_out,
    grad_out,
    seq_lengths,
    group_ids,
    rewards,
    wide_params,
    wide_moments,
    head_params,
    head_moments,
    key_value_adapters,
    kv_moments,
    base_query,
    frozen_key_rows,
    rotary_rows,
    rollout_group_order,
):
    count = lax.axis_size("dp")
    tensor_pos = lax.axis_index("tensor")
    layers, tokens, model_width = acts.shape
    wide_rows = wide_params.shape[1]
    rank = wide_params.shape[2] // 4
    heads, share_rows = head_params.shape[1:3]
    kv_heads = key_value_adapters.shape[1]
    all_heads = heads + kv_heads
    base_there = swap_core(base_query)
    frozen_there = swap_core(frozen_key_rows)

    wide_bf = wide_params.astype(jnp.bfloat16).reshape(-1, 4 * rank)
    head_bf = jnp.concatenate([head_params, key_value_adapters], axis=1).astype(jnp.bfloat16)
    wide_all, head_all = gather_dp([wide_bf, head_bf.reshape(-1, 2 * rank)], [], count, False, 0)
    wide_all = wide_all.reshape(count, layers, wide_rows, 4 * rank)
    head_all = head_all.reshape(count, layers, all_heads, share_rows, 2 * rank)
    head_all = head_all.transpose(1, 2, 0, 3, 4).reshape(layers, all_heads, -1, 2 * rank)

    def own_columns(value):
        split = value.reshape(layers, tokens, count, 2, wide_rows)
        return lax.dynamic_index_in_dim(split, tensor_pos, 3, keepdims=False).reshape(
            layers, tokens, count * wide_rows
        )

    x_own, out_own = own_columns(acts), own_columns(grad_out)
    weight_col = token_weights(seq_lengths, group_ids, rewards, tokens)[:, None]
    dot = functools.partial(jnp.dot, preferred_element_type=jnp.float32)
    parts = []
    for layer in range(layers):
        wide = wide_all[:, layer].reshape(-1, 4 * rank)
        flat_head = head_all[layer, :heads].reshape(-1, 2 * rank)
        flat_kv = head_all[layer, heads:].reshape(-1, 2 * rank)
        parts.append(
            jnp.concatenate(
                [
                    dot(x_own[layer], wide)[:, : 3 * rank],
                    dot(out_own[layer], wide)[:, 3 * rank :],
                    dot(grad_query[layer], flat_head)[:, :rank],
                    dot(attn_out[layer], flat_head)[:, rank:],
                    dot(keyvalue_gradient[layer, :, 0], flat_kv)[:, :rank],
                    dot(keyvalue_gradient[layer, :, 1], flat_kv)[:, rank:],
                ],
                axis=1,
            )
        )
    part = jnp.stack(parts)
    low = (weight_col * (part + swap_core(part))).astype(jnp.bfloat16)
    wide_chunks, head_chunks = [], []
    for layer in range(layers):
        hidden = low[layer, :, : 3 * rank]
        gate_output = low[layer, :, 3 * rank : 4 * rank]
        gate_query = low[layer, :, 4 * rank : 5 * rank]
        hidden_output = low[layer, :, 5 * rank : 6 * rank]
        gate_kv = low[layer, :, 6 * rank :]
        none = jnp.zeros((tokens, rank), jnp.bfloat16)
        wide_grad = contracted_rows(
            x_own[layer], jnp.concatenate([gate_query, gate_kv, none], axis=1)
        ) + contracted_rows(
            out_own[layer], jnp.concatenate([none, none, none, hidden_output], axis=1)
        )
        head_grad = contracted_rows(
            grad_query[layer], jnp.concatenate([hidden[:, :rank], none], axis=1)
        ) + contracted_rows(attn_out[layer], jnp.concatenate([none, gate_output], axis=1))
        kv_grad = contracted_rows(
            keyvalue_gradient[layer, :, 0],
            jnp.concatenate([hidden[:, rank : 2 * rank], none], axis=1),
        ) + contracted_rows(
            keyvalue_gradient[layer, :, 1],
            jnp.concatenate([none, hidden[:, 2 * rank :]], axis=1),
        )
        wide_chunks.append((adapter_scale * wide_grad).astype(jnp.bfloat16))
        head_chunks.append(
            jnp.concatenate(
                [
                    (adapter_scale * grad).astype(jnp.bfloat16).reshape(-1, count, share_rows, 2 * rank)
                    for grad in (head_grad, kv_grad)
                ]
            ).transpose(1, 0, 2, 3)
        )
    wide_send = jnp.stack(
        [chunk.reshape(count, wide_rows, 4 * rank) for chunk in wide_chunks], axis=1
    ).reshape(count, -1, 4 * rank)
    head_send = jnp.stack(head_chunks, axis=1).reshape(count, -1, 2 * rank)
    wide_sum, head_sum = scatter_dp([wide_send, head_send], count, 1)
    wide_grad = wide_sum.reshape(wide_params.shape)
    head_sum = head_sum.reshape(layers, all_heads, share_rows, 2 * rank)
    new_wide, new_wide_moments = adamw(wide_params, wide_moments, wide_grad)
    new_head, new_head_moments = adamw(head_params, head_moments, head_sum[:, :heads])
    new_kv, new_kv_moments = adamw(key_value_adapters, kv_moments, head_sum[:, heads:])

    up_own = jnp.concatenate([new_head[..., :rank], new_kv[..., :rank]], axis=1).astype(jnp.bfloat16)
    down_own = new_wide[..., : 2 * rank].astype(jnp.bfloat16)
    up_here, up_there, down_there = gather_dp(
        [up_own.reshape(-1, 2 * rank)], [down_own.reshape(-1, 2 * rank)], count, True, 2
    )
    down_there = down_there.reshape(down_own.shape)
    first = tensor_pos == 0
    rank_down = jnp.concatenate(
        [jnp.where(first, down_own, down_there), jnp.where(first, down_there, down_own)], axis=1
    )

    slot_groups = kv_heads
    group_slots = tensor_pos * slot_groups + jnp.arange(slot_groups, dtype=jnp.int32)
    source_groups = jnp.take(rollout_group_order, group_slots)
    away = (source_groups // slot_groups != tensor_pos).astype(jnp.int32)
    near = (source_groups % slot_groups).astype(jnp.int32)

    both = jnp.stack([up_here, up_there]).reshape(2, count, layers, all_heads, share_rows, rank)

    def picked(low_head, amount):
        grouped = both[:, :, :, low_head : low_head + amount].reshape(
            2, count, layers, slot_groups, amount // slot_groups, share_rows, rank
        )
        rows = [
            lax.dynamic_index_in_dim(
                lax.dynamic_index_in_dim(grouped, away[slot], 0, keepdims=False),
                near[slot],
                2,
                keepdims=False,
            )
            for slot in range(slot_groups)
        ]
        stacked = jnp.stack(rows, axis=2)
        return stacked.transpose(1, 2, 3, 0, 4, 5).reshape(layers, amount, -1, rank)

    mix = (rotary_rows[:, None] == jnp.arange(rotary_rows.shape[0], dtype=jnp.int32)[None, :]).astype(
        jnp.bfloat16
    )
    merged_query = merge(
        base_query, base_there, picked(0, heads), rank_down, mix, away, near, 0
    )
    merged_key = merge(
        frozen_key_rows, frozen_there, picked(heads, kv_heads), rank_down, mix, away, near, rank
    )
    return (
        new_wide,
        new_wide_moments,
        new_head,
        new_head_moments,
        new_kv,
        new_kv_moments,
        merged_query,
        merged_key,
    )


def solution(mesh):
    placed = (
        P("groups", "dp", None),
        P("groups", "dp", "tensor"),
        P("groups", "dp", None, "tensor"),
        P("groups", "dp", "tensor"),
        P("groups", "dp", None),
        P("dp", "groups"),
        P("dp", "groups"),
        P("dp", "groups"),
        P("groups", ("dp", "tensor"), None),
        P(None, "groups", ("dp", "tensor"), None),
        P("groups", "tensor", "dp", None),
        P(None, "groups", "tensor", "dp", None),
        P("groups", "tensor", "dp", None),
        P(None, "groups", "tensor", "dp", None),
        P(None, "tensor", None, "dp"),
        P(None, "tensor", None, "dp"),
        P(),
        P(),
    )
    return jax.shard_map(
        body,
        mesh=mesh,
        in_specs=placed,
        out_specs=(
            P("groups", ("dp", "tensor"), None),
            P(None, "groups", ("dp", "tensor"), None),
            P("groups", "tensor", "dp", None),
            P(None, "groups", "tensor", "dp", None),
            P("groups", "tensor", "dp", None),
            P(None, "groups", "tensor", "dp", None),
            P("groups", "tensor", None, "dp"),
            P("groups", "tensor", None, "dp"),
        ),
        check_vma=False,
    )
```

time: 629 us -> 252 us (0.40)
  waiting for transfers between devices: 311 us -> 0.01 us
  Pallas kernels: 0 us -> 146 us
  blocking collectives: 65.4 us -> 0 us
  local copies, waits for them, and re-layouts: 115 us -> 52.1 us
  matrix products: 65.3 us -> 25.2 us
  other arithmetic: 50.5 us -> 17.1 us
    reduce_scatter x2 -> x0, waiting for transfers between devices: 205 us -> none  [the longest x1 138 us: body(): lax.psum_scatter(wide_stack, 'dp', scatter_dimension=1, tiled=True)]
    pallas_call x0 -> x5, Pallas kernels: none -> 146 us  [the longest x2 74 us: gather_dp(): pl.pallas_call(functools.partial(gather_kernel, count, pieces, share, swa...]
    all_gather x5 -> x0, waiting for transfers between devices: 90.4 us -> none  [the longest x1 42.4 us: body(): lax.all_gather(wide_params.astype(jnp.bfloat16), ('dp', 'tensor'), axis=1...]
    all_gather x3 -> x0, blocking collectives: 65.4 us -> none  [the longest x1 32.6 us: body(): lax.all_gather(key_value_adapters.astype(jnp.bfloat16), 'dp', axis=2, til...]
    gather x10 -> x0, local copies, waits for them, and re-layouts: 39.1 us -> none  [the longest x2 12.5 us: merge_local(): jnp.take(jnp.take(base_rows, head_index, axis=1), row_order, axis=2)]
    dot_general x12, matrix products: 37.4 us -> 11.7 us  [the longest x2 3.01 us: body(): dot(grad_query[layer], flat_head)[:, :rank]]
    select_n x11 -> x2, other arithmetic: 20 us -> 1 us  [the longest x1 0.98 us: body(): jnp.where(first, down_own, down_there)]
    concatenate x12 -> x3, local copies, waits for them, and re-layouts: 18.1 us -> 0.68 us  [the longest x1 0.66 us: body(): jnp.concatenate([gate_query, gate_kv, none], axis=1)]
  transfers between devices with their start and end apart: 9 -> 3, of which waited for: 7 -> 0; matrix products, arithmetic and copies ran while one was open for 31% -> 20% of each run, Pallas kernels for 0% -> 30%
where the time goes in v1:
time: 252 us; the launch traced here: 250 us
  Pallas kernels  146 us (58%)
  local copies, waits for them, and re-layouts  52.1 us (21%)
  matrix products  25.2 us (10%)
  other arithmetic  17.1 us (7%)
  between operations  9.14 us (4%)
    pallas_call x2, Pallas kernels, gather_dp(): pl.pallas_call(functools.partial(gather_kernel, count, pieces, share, swa...  74 us
    pallas_call x1, Pallas kernels, scatter_dp(): pl.pallas_call(functools.partial(scatter_kernel, count, pieces), out_shap...  50.6 us
    pallas_call x2, Pallas kernels, merge(): pl.pallas_call(functools.partial(merge_kernel, first, heads), out_shape=j...  21.2 us
    unnamed x123, local copies, waits for them, and re-layouts  21.2 us
    dot_general x12, matrix products, contracted_rows(): lax.dot_general(left, right, (((0,), (0,)), ((), ())), preferred_element_...  13.5 us
    another operation x3, local copies, waits for them, and re-layouts, body(): jnp.stack([up_here, up_there])  8.31 us
    convert_element_type x4, local copies, waits for them, and re-layouts, body(): (adapter_scale * grad).astype(jnp.bfloat16)  6.19 us
  transfers between devices with their start and end apart: 3, of which 0 were waited for; matrix products, arithmetic and copies ran while one was open for 20% of the time, Pallas kernels for 30%

profile of v1, /device:TPU:0, one launch (start us, length us, event | category | flops | bytes accessed | tf_op | source)
XLA Modules:
  0.0 250.1 jit_solution(9108304446168881250)
XLA Ops:
  2.5 1.8 convert_element_type.70
  5.0 52.0 %gather_pieces.2 = (bf16[8,512,256]{2,1,0:T(8,128)(2,1)}, bf16[8,1088,128]{2,1,0:T(8,128)(2,1)}) custom-call(bf16[512,256]{1,0:T(8,128)(2,1)} %bitcast.272, bf16[1088,128]{1,0:T(8,128)(2,1)} %bitcast.271), custom_call_target="tpu_custom_call" | custom-call | tf_op jit(solution)/shard_map/gather_pieces/pallas_call | solution.py:211
  57.1 2.4 copy.72
  60.4 1.3 copy-done.8
  61.7 1.5 fusion.32
  63.2 1.5 fusion.35
  64.7 1.5 fusion.38
  66.2 1.5 fusion.41
  67.7 6.3 %copy.70 = bf16[2,256,4096]{1,2,0:T(8,128)(2,1)} copy(bf16[2,256,4096]{2,1,0:T(8,128)(2,1)} %param.18) | data formatting | bytes 8388608 | tf_op args[0]
  74.1 6.5 %copy.71 = bf16[2,256,4096]{1,2,0:T(8,128)(2,1)} copy(bf16[2,256,4096]{2,1,0:T(8,128)(2,1)} %param.22) | data formatting | bytes 8388608 | tf_op args[4]
  80.5 1.5 fusion.115
  86.3 2.6 %constant_dynamic-slice_fusion = (bf16[1,256,8,1,256]{1,4,3,2,0:T(8,128)(2,1)S(1)}, bf16[1,256,8,1,256]{1,4,3,2,0:T(8,128)(2,1)S(1)}, bf16[1,256,8,1,256]{1,4,3,...) fusion(bf16[2,256,8,2,256]{1,4,3,2,0:T(8,128)(2,1)} %bitcast.243, s32[]{:T(128)S(6)} %select_n.76, s32[]{:T(128)S(6)} %add.220, ...), kind=kLoop, calls=%fused_computation.176 | loop fusion | bytes 8388616 | tf_op jit(solution)/shard_map/slice | solution.py:482
  105.0 1.7 multiply_convert_fusion
  107.5 2.2 fusion.20
  110.3 1.5 fusion.5
  111.8 2.2 copy.79
  115.9 1.8 fusion.48
  117.7 1.6 copy.80
  119.3 2.2 fusion.13
  122.1 1.5 fusion.4
  123.5 2.3 copy.81
  126.0 1.1 fusion.49
  127.2 1.4 maximum_bitcast_fusion
  133.3 50.6 %sum_to_owners.1 = (f32[512,256]{1,0:T(8,128)S(1)}, f32[1088,128]{1,0:T(8,128)S(1)}) custom-call(bf16[8,512,256]{2,1,0:T(8,128)(2,1)S(1)} %bitcast.235, bf16[8,1088,128]{2,1,0:T(8,128)(2,1)S(1)} %bitcast.234), custom_call_target="tpu_custom_call" | custom-call | tf_op jit(solution)/shard_map/sum_to_owners/pallas_call | solution.py:342
  184.0 1.4 fusion.75
  187.1 1.6 multiply_subtract_fusion.1
  189.4 22.0 %gather_pieces.3 = (bf16[8,544,128]{2,1,0:T(8,128)(2,1)}, bf16[8,544,128]{2,1,0:T(8,128)(2,1)}, bf16[512,128]{1,0:T(8,128)(2,1)}) custom-call(bf16[544,128]{1,0:T(8,128)(2,1)} %convert_element_type.85.refs_0_, bf16[512,128]{1,0:T(8,128)(2,1)} %bitcast.281), custom_call_target="tpu_custom_call" | custom-call | tf_op jit(solution)/shard_map/gather_pieces/pallas_call | solution.py:211
  211.5 3.9 %stack.77 = bf16[1,8,2,34,16,64]{5,4,3,2,1,0:T(8,128)(2,1)} reshape(bf16[8,544,128]{2,1,0:T(8,128)(2,1)} %get-tuple-element.19) | data formatting | bytes 2228224 | tf_op jit(solution)/shard_map/stack | solution.py:553
  215.3 3.9 %stack.78 = bf16[1,8,2,34,16,64]{5,4,3,2,1,0:T(8,128)(2,1)} reshape(bf16[8,544,128]{2,1,0:T(8,128)(2,1)} %get-tuple-element.20) | data formatting | bytes 2228224 | tf_op jit(solution)/shard_map/stack | solution.py:553
  219.2 2.2 constant_dynamic-update-slice_fusion.1
  225.5 3.0 %merged_rows.3 = bf16[2,2,128,512]{3,2,1,0:T(8,128)(2,1)} custom-call(s32[2]{0:T(128)S(1)} %compare_convert_fusion.1.away_ref, s32[2]{0:T(128)S(1)} %get-tuple-element.24.near_ref, bf16[128,128]{1,0:T(8,128)(2,1)S(1)} %fusion.89.mix, bf16[2,2,128,512]{3,2,1,0:T(8,128)(2,1)S(1)} %copy-done.2, bf16[2,2,128,512]{3,2,1,0:T(8,128)(2,1)S(1)} %collective-permute-done.2.there, ...), custom_call_target="tpu_custom_call" | custom-call | tf_op jit(solution)/shard_map/merged_rows/pallas_call | solution.py:402
  231.8 18.2 %merged_rows.2 = bf16[2,32,128,512]{3,2,1,0:T(8,128)(2,1)} custom-call(s32[2]{0:T(128)S(1)} %compare_convert_fusion.1.away_ref, s32[2]{0:T(128)S(1)} %get-tuple-element.24.near_ref, bf16[128,128]{1,0:T(8,128)(2,1)S(1)} %fusion.89.mix, bf16[2,32,128,512]{3,2,1,0:T(8,128)(2,1)} %here.2, bf16[2,32,128,512]{3,2,1,0:T(8,128)(2,1)} %collective-permute-done.1.there, ...), custom_call_target="tpu_custom_call" | custom-call | tf_op jit(solution)/shard_map/merged_rows/pallas_call | solution.py:402
  (194 shorter events, 34.3 us)
Async XLA Ops:
  0.6 93.6 %copy-start = (s32[4]{0:T(128)S(1)}, s32[4]{0:T(128)}, u32[]{:S(2)}) copy-start(s32[4]{0:T(128)} %param.35) | copy-start | bytes 52
  57.0 6.2 %copy-start.9 = (bf16[2,256,4096]{2,1,0:T(8,128)(2,1)S(1)}, bf16[2,256,4096]{2,1,0:T(8,128)(2,1)}, u32[]{:S(2)}) copy-start(bf16[2,256,4096]{2,1,0:T(8,128)(2,1)} %param.21) | copy-start | bytes 12582916
  59.5 2.2 copy-start.8
  74.1 6.5 %copy-start.19 = (bf16[8,512,256]{2,1,0:T(8,128)(2,1)S(1)}, bf16[8,512,256]{2,1,0:T(8,128)(2,1)}, u32[]{:S(2)}) copy-start(bf16[8,512,256]{2,1,0:T(8,128)(2,1)} %get-tuple-element.15) | copy-start | bytes 6291460
  82.8 3.5 %copy-start.28 = (bf16[1,256,1,256]{3,2,1,0:T(2,128)(2,1)}, bf16[1,256,1,256]{3,2,1,0:T(2,128)(2,1)S(1)}, u32[]{:S(2)}) copy-start(bf16[1,256,1,256]{3,2,1,0:T(2,128)(2,1)S(1)} %get-tuple-element.58) | copy-start | bytes 393220
  82.8 3.5 %copy-start.29 = (bf16[1,256,1,256]{3,2,1,0:T(2,128)(2,1)}, bf16[1,256,1,256]{3,2,1,0:T(2,128)(2,1)S(1)}, u32[]{:S(2)}) copy-start(bf16[1,256,1,256]{3,2,1,0:T(2,128)(2,1)S(1)} %get-tuple-element.59) | copy-start | bytes 393220
  86.3 2.6 %copy-start.15 = (bf16[8,1,256,256]{3,2,1,0:T(8,128)(2,1)S(1)}, bf16[8,1,256,256]{3,2,1,0:T(8,128)(2,1)}, u32[]{:S(2)}) copy-start(bf16[8,1,256,256]{3,2,1,0:T(8,128)(2,1)} %get-tuple-element.36) | copy-start | bytes 3145732
  88.9 1.8 copy-start.4
  88.9 2.2 copy-start.14
  90.6 1.8 copy-start.24
  91.7 1.9 copy-start.2
  91.7 9.5 %copy-start.55 = (s32[1,8]{1,0:T(1,128)S(1)}, s32[1,8]{1,0:T(1,128)}, u32[]{:S(2)}) copy-start(s32[1,8]{1,0:T(1,128)} %param.23) | copy-start | bytes 100
  91.7 12.9 %copy-start.51 = (f32[1,8]{1,0:T(1,128)S(1)}, f32[1,8]{1,0:T(1,128)}, u32[]{:S(2)}) copy-start(f32[1,8]{1,0:T(1,128)} %param.25) | copy-start | bytes 100
  91.7 12.9 %copy-start.52 = (s32[1,8]{1,0:T(1,128)S(1)}, s32[1,8]{1,0:T(1,128)}, u32[]{:S(2)}) copy-start(s32[1,8]{1,0:T(1,128)} %param.24) | copy-start | bytes 100
  91.7 13.1 %copy-start.54 = (s32[128]{0:T(128)S(1)}, s32[128]{0:T(128)}, u32[]{:S(2)}) copy-start(s32[128]{0:T(128)} %param.34) | copy-start | bytes 1540
  93.6 13.9 %copy-start.50 = (pred[128]{0:T(512)(128)(4,1)S(1)}, pred[128]{0:T(512)(128)(4,1)}, u32[]{:S(2)}) copy-start(pred[128]{0:T(512)(128)(4,1)} %constant.238.clone.1) | copy-start | bytes 388
  93.6 11.4 %collective-permute-start = (f32[2,256,512]{1,2,0:T(8,128)}, f32[2,256,512]{1,2,0:T(8,128)}, u32[]{:S(2)}, u32[]{:S(2)}) collective-permute-start(f32[2,256,512]{1,2,0:T(8,128)} %pad_maximum_fusion.3), channel_id=1, source_target_pairs={{0,1},{1,0},{2,3},{3,2},{4,5},{5,4},{6,7},{7,6},{8,9},{9,8},{10,11... | collective-permute-start | bytes 3145736 | tf_op jit(solution)/shard_map/ppermute | solution.py:423
  93.6 131.8 %collective-permute-start.2 = (bf16[2,2,128,512]{3,2,1,0:T(8,128)(2,1)S(1)}, bf16[2,2,128,512]{3,2,1,0:T(8,128)(2,1)S(1)}, u32[]{:S(2)}, u32[]{:S(2)}) collective-permute-start(bf16[2,2,128,512]{3,2,1,0:T(8,128)(2,1)S(1)} %copy-done.2), channel_id=1, source_target_pairs={{0,1},{1,0},{2,3},{3,2},{4,5},{5,4},{6,7},{7,6},{8,9},{9,8},{10,11... | collective-permute-start | bytes 1572872 | tf_op jit(solution)/shard_map/ppermute | solution.py:423
  94.1 137.7 %collective-permute-start.1 = (bf16[2,32,128,512]{3,2,1,0:T(8,128)(2,1)}, bf16[2,32,128,512]{3,2,1,0:T(8,128)(2,1)}, u32[]{:S(2)}, u32[]{:S(2)}) collective-permute-start(bf16[2,32,128,512]{3,2,1,0:T(8,128)(2,1)} %here.2), channel_id=1, source_target_pairs={{0,1},{1,0},{2,3},{3,2},{4,5},{5,4},{6,7},{7,6},{8,9},{9,8},{10,11... | collective-permute-start | bytes 25165832 | tf_op jit(solution)/shard_map/ppermute | solution.py:423
  107.5 2.2 copy-start.32
  107.5 2.9 %copy-start.10 = (bf16[2,256,4096]{2,1,0:T(8,128)(2,1)S(1)}, bf16[2,256,4096]{2,1,0:T(8,128)(2,1)}, u32[]{:S(2)}) copy-start(bf16[2,256,4096]{2,1,0:T(8,128)(2,1)} %param.21) | copy-start | bytes 12582916
  119.3 2.8 %copy-start.11 = (bf16[2,256,4096]{2,1,0:T(8,128)(2,1)S(1)}, bf16[2,256,4096]{2,1,0:T(8,128)(2,1)}, u32[]{:S(2)}) copy-start(bf16[2,256,4096]{2,1,0:T(8,128)(2,1)} %param.21) | copy-start | bytes 12582916
  119.3 2.8 %copy-start.41 = (bf16[256,64]{0,1:T(8,128)(2,1)S(1)}, bf16[256,64]{0,1:T(8,128)(2,1)}, u32[]{:S(2)}) copy-start(bf16[256,64]{0,1:T(8,128)(2,1)} %get-tuple-element.47) | copy-start | bytes 98308
  133.3 50.7 %copy-start.17 = (f32[2,32,16,128]{3,2,1,0:T(8,128)S(1)}, f32[2,32,16,128]{3,2,1,0:T(8,128)}, u32[]{:S(2)}) copy-start(f32[2,32,16,128]{3,2,1,0:T(8,128)} %param.28) | copy-start | bytes 1572868
  133.3 50.7 %copy-start.27 = (f32[2,2,32,16,128]{4,3,2,1,0:T(8,128)S(1)}, f32[2,2,32,16,128]{4,3,2,1,0:T(8,128)}, u32[]{:S(2)}) copy-start(f32[2,2,32,16,128]{4,3,2,1,0:T(8,128)} %param.29) | copy-start | bytes 3145732
  186.2 29.2 %copy-start.44 = (f32[2,2,16,128]{3,2,1,0:T(8,128)}, f32[2,2,16,128]{3,2,1,0:T(8,128)S(1)}, u32[]{:S(2)}) copy-start(f32[2,2,16,128]{3,2,1,0:T(8,128)S(1)} %get-tuple-element.45) | copy-start | bytes 98308
  188.7 30.5 %copy-start.25 = (f32[2,256,256]{2,1,0:T(8,128)}, f32[2,256,256]{2,1,0:T(8,128)S(1)}, u32[]{:S(2)}) copy-start(f32[2,256,256]{2,1,0:T(8,128)S(1)} %multiply_subtract_fusion.1) | copy-start | bytes 1572868
  219.2 2.3 copy-start.3
  224.1 5.0 %copy-start.21 = (f32[1,2,32,16,128]{4,3,2,1,0:T(8,128)S(1)}, f32[1,2,32,16,128]{4,3,2,1,0:T(8,128)}, u32[]{:S(2)}) copy-start(f32[1,2,32,16,128]{4,3,2,1,0:T(8,128)} %get-tuple-element.38) | copy-start | bytes 1572868
  224.1 5.0 %copy-start.22 = (f32[1,2,32,16,128]{4,3,2,1,0:T(8,128)S(1)}, f32[1,2,32,16,128]{4,3,2,1,0:T(8,128)}, u32[]{:S(2)}) copy-start(f32[1,2,32,16,128]{4,3,2,1,0:T(8,128)} %get-tuple-element.39) | copy-start | bytes 1572868
  225.4 4.7 %copy-start.12 = (f32[2,2,256,256]{3,2,1,0:T(8,128)S(1)}, f32[2,2,256,256]{3,2,1,0:T(8,128)}, u32[]{:S(2)}) copy-start(f32[2,2,256,256]{3,2,1,0:T(8,128)} %param.27) | copy-start | bytes 3145732
  231.8 18.2 %copy-start.1 = (s32[4]{0:T(128)S(1)}, s32[4]{0:T(128)}, u32[]{:S(2)}) copy-start(s32[4]{0:T(128)} %param.35) | copy-start | bytes 52
  (27 other events, 33.9 us)

commit v2 on v1

--- a/solution.py
+++ b/solution.py
@@ -94,11 +94,19 @@
     send_right, send_left, send_row, recv, local_sem = take(5)
     send_core, recv_core = take(2) if share else (None, None)
     send_swap, recv_swap = take(2) if swaps else (None, None)
+    sems = (send_right, send_left, send_row, recv, local_sem, send_core, recv_core, send_swap, recv_swap)
+    exchange(count, ins, swap_ins, outs, others, swap_outs, sems, share, False, None)
+
+
+def exchange(count, ins, swap_ins, outs, others, swap_outs, sems, share, greet_core, use):
+    pieces, swaps = len(ins), len(swap_ins)
+    (send_right, send_left, send_row, recv, local_sem, send_core, recv_core, send_swap, recv_swap) = sems
+    use = use or (lambda p, slot: None)
     me, z, y, m = place(count)
     row_mate = {"dp": me + 1 - 2 * y}
     core_mate = {"tensor": 1 - lax.axis_index("tensor")}
     has_left, has_right = z > 0, z < m - 1
-    greet(z, m, [row_mate] + ([core_mate] if share or swaps else []))
+    greet(z, m, [row_mate] + ([core_mate] if share or swaps or greet_core else []))
 
     def right(p, src, k):
         slot = (z - k) * 2 + y
@@ -137,6 +145,9 @@
         if share:
             to_core(p, own[p], me).start()
         pltpu.make_async_copy(ins[p], outs[p].at[me], local_sem.at[p]).start()
+    for p in range(pieces):
+        pltpu.make_async_copy(ins[p], outs[p].at[me], local_sem.at[p]).wait()
+        use(p, me)
 
     for k in range(1, m):
         for p in range(pieces):
@@ -153,6 +164,7 @@
                 across(p, held[p], z - k).start()
                 if share:
                     to_core(p, held[p], slot).start()
+                use(p, slot)
 
             @pl.when(z + k < m)
             def _():
@@ -166,6 +178,7 @@
                 across(p, held[p], z + k).start()
                 if share:
                     to_core(p, held[p], slot).start()
+                use(p, slot)
 
     far = 1 - y
     for zz in range(m):
@@ -174,8 +187,8 @@
             arrive(p, slot)
             if share:
                 to_core(p, held[p], slot).start()
+            use(p, slot)
     for p in range(pieces):
-        pltpu.make_async_copy(ins[p], outs[p].at[me], local_sem.at[p]).wait()
         for zz in range(m):
             across(p, held[p], zz).wait_send()
         for k in range(m):
@@ -219,6 +232,202 @@
     )(*arrays, *swapped)
 
 
+def column_copy(array, held, sems, slot, width):
+    first = pl.multiple_of((slot * 2 + lax.axis_index("tensor")) * width, width)
+    return pltpu.make_async_copy(array.at[:, :, pl.ds(first, width)], held.at[slot], sems.at[slot])
+
+
+def product(left, right, contract=1):
+    return lax.dot_general(
+        left, right, (((contract,), (0,)), ((), ())), preferred_element_type=jnp.float32
+    )
+
+
+def forward_kernel(
+    count,
+    share_rows,
+    wide_in,
+    head_in,
+    acts,
+    grad_out,
+    grad_query,
+    attn_out,
+    key_grad,
+    value_grad,
+    weights,
+    out,
+    wide_all,
+    head_all,
+    x_held,
+    out_held,
+    query_held,
+    attn_held,
+    x_total,
+    out_total,
+    query_total,
+    attn_total,
+    part,
+    part_there,
+    send_right,
+    send_left,
+    send_row,
+    recv,
+    local_sem,
+    x_sem,
+    out_sem,
+    query_sem,
+    attn_sem,
+    core_send,
+    core_recv,
+):
+    layers, tokens, _ = acts.shape
+    width = wide_in.shape[0] // layers
+    size = count * share_rows
+    heads = grad_query.shape[2] // size
+    all_heads = head_in.shape[0] // (layers * share_rows)
+    core_mate = {"tensor": 1 - lax.axis_index("tensor")}
+    for slot in range(count):
+        column_copy(acts, x_held, x_sem, slot, width).start()
+        column_copy(grad_out, out_held, out_sem, slot, width).start()
+    for layer in range(layers):
+        pltpu.make_async_copy(grad_query.at[layer], query_held.at[layer], query_sem.at[layer]).start()
+        pltpu.make_async_copy(attn_out.at[layer], attn_held.at[layer], attn_sem.at[layer]).start()
+    for total in (x_total, out_total, query_total, attn_total):
+        total[...] = jnp.zeros_like(total)
+
+    def use(p, slot):
+        if p == 0:
+            column_copy(acts, x_held, x_sem, slot, width).wait()
+            column_copy(grad_out, out_held, out_sem, slot, width).wait()
+            for layer in range(layers):
+                factors = wide_all[slot, layer * width : (layer + 1) * width, :]
+                x_total[layer] += product(x_held[slot, layer], factors)
+                out_total[layer] += product(out_held[slot, layer], factors)
+
+    sems = (send_right, send_left, send_row, recv, local_sem, None, None, None, None)
+    exchange(count, [wide_in, head_in], [], [wide_all, head_all], [], [], sems, False, True, use)
+
+    span = max(1, 16 // share_rows)
+
+    def head_rows(layer, head):
+        start = pl.multiple_of((layer * all_heads + head) * share_rows, span * share_rows)
+        units = [head_all[slot, pl.ds(start, span * share_rows), :] for slot in range(count)]
+        if span == 1:
+            return jnp.concatenate(units, axis=0)
+        units = [unit.astype(jnp.float32) for unit in units]
+        rows = [unit[j * share_rows : (j + 1) * share_rows] for j in range(span) for unit in units]
+        return jnp.concatenate(rows, axis=0).astype(head_all.dtype)
+
+    half = head_in.shape[1]
+    low_half = lax.broadcasted_iota(jnp.int32, (tokens, half), 1) < half // 2
+    group = 4 if heads % 4 == 0 else 1
+
+    def swap(layer):
+        return remote(
+            part.at[layer], part_there.at[layer], core_send.at[layer], core_recv.at[layer], core_mate
+        )
+
+    for layer in range(layers):
+        pltpu.make_async_copy(grad_query.at[layer], query_held.at[layer], query_sem.at[layer]).wait()
+        pltpu.make_async_copy(attn_out.at[layer], attn_held.at[layer], attn_sem.at[layer]).wait()
+
+        def step(i, carry):
+            factors = jnp.concatenate(
+                [head_rows(layer, i * group + j) for j in range(0, group, span)], axis=0
+            )
+            columns = pl.ds(pl.multiple_of(i * group * size, group * size), group * size)
+            query_total[layer] += product(query_held[layer, :, columns], factors)
+            attn_total[layer] += product(attn_held[layer, :, columns], factors)
+            return carry
+
+        lax.fori_loop(0, heads // group, step, 0)
+        kv_factors = jnp.concatenate(
+            [head_rows(layer, heads + j) for j in range(0, all_heads - heads, span)], axis=0
+        )
+        part[layer, :, :half] = x_total[layer, :, :half]
+        part[layer, :, half : 2 * half] = jnp.where(
+            low_half, x_total[layer, :, half:], out_total[layer, :, half:]
+        )
+        part[layer, :, 2 * half : 3 * half] = jnp.where(
+            low_half, query_total[layer], attn_total[layer]
+        )
+        part[layer, :, 3 * half :] = jnp.where(
+            low_half, product(key_grad[layer], kv_factors), product(value_grad[layer], kv_factors)
+        )
+        swap(layer).start()
+
+    for layer in range(layers):
+        swap(layer).wait()
+
+        def piece(k):
+            columns = slice(k * half, (k + 1) * half)
+            return weights[...] * (part[layer, :, columns] + part_there[layer, :, columns])
+
+        hidden_qk, hidden_v_out, query_outer, key_value = (piece(k) for k in range(4))
+        zero = jnp.zeros((tokens, half), jnp.float32)
+
+        def turned(value):
+            return pltpu.roll(value, half // 2, 1)
+
+        columns = [
+            jnp.where(low_half, query_outer, turned(key_value)),
+            jnp.where(low_half, turned(key_value), zero),
+            zero,
+            jnp.where(low_half, zero, query_outer),
+            jnp.where(low_half, hidden_qk, zero),
+            jnp.where(low_half, zero, hidden_v_out),
+            jnp.where(low_half, turned(hidden_qk), zero),
+            jnp.where(low_half, zero, turned(hidden_v_out)),
+        ]
+        for k, value in enumerate(columns):
+            out[layer, :, k * half : (k + 1) * half] = value.astype(jnp.bfloat16)
+
+
+def forward(wide, head, acts, grad_out, grad_query, attn_out, key_grad, value_grad, weights, count, share_rows, collective_id):
+    layers, tokens, _ = acts.shape
+    width = wide.shape[0] // layers
+    half = head.shape[1]
+    m = count // 2
+    dma = pltpu.SemaphoreType.DMA
+    anywhere, vmem = pl.BlockSpec(memory_space=pl.ANY), pl.BlockSpec(memory_space=pltpu.VMEM)
+    total = lambda columns: pltpu.VMEM((layers, tokens, columns), jnp.float32)
+    return pl.pallas_call(
+        functools.partial(forward_kernel, count, share_rows),
+        out_shape=jax.ShapeDtypeStruct((layers, tokens, 8 * half), jnp.bfloat16),
+        in_specs=[vmem] * 2 + [anywhere] * 4 + [vmem] * 3,
+        out_specs=vmem,
+        scratch_shapes=[
+            pltpu.VMEM((count,) + wide.shape, wide.dtype),
+            pltpu.VMEM((count,) + head.shape, head.dtype),
+            pltpu.VMEM((count, layers, tokens, width), acts.dtype),
+            pltpu.VMEM((count, layers, tokens, width), acts.dtype),
+            pltpu.VMEM(grad_query.shape, grad_query.dtype),
+            pltpu.VMEM(attn_out.shape, attn_out.dtype),
+            total(2 * half),
+            total(2 * half),
+            total(half),
+            total(half),
+            total(4 * half),
+            total(4 * half),
+            dma((2, m)),
+            dma((2, m)),
+            dma((2, m)),
+            dma((2, count)),
+            dma((2,)),
+            dma((count,)),
+            dma((count,)),
+            dma((layers,)),
+            dma((layers,)),
+            dma((layers,)),
+            dma((layers,)),
+        ],
+        compiler_params=pltpu.CompilerParams(
+            collective_id=collective_id, has_side_effects=True, vmem_limit_bytes=44 * 2**20
+        ),
+        name="gather_and_low_products",
+    )(wide, head, acts, grad_out, grad_query, attn_out, key_grad, value_grad, weights)
+
+
 def add_rows(dst, terms):
     def step(i, carry):
         rows = pl.ds(pl.multiple_of(i * ROW_STEP, ROW_STEP), ROW_STEP)
@@ -231,16 +440,91 @@
     lax.fori_loop(0, dst.shape[0] // ROW_STEP, step, 0)
 
 
-def scatter_kernel(count, pieces, *refs):
-    refs = list(refs)
-    take = lambda k: [refs.pop(0) for _ in range(k)]
-    ins, outs = take(pieces), take(pieces)
-    from_row, from_left, from_right, leaving = take(pieces), take(pieces), take(pieces), take(pieces)
-    row_send, row_recv, line_send, left_recv, right_recv = take(5)
+def backward_kernel(
+    count,
+    share_rows,
+    acts,
+    grad_out,
+    grad_query,
+    attn_out,
+    key_grad,
+    value_grad,
+    low,
+    wide_out,
+    head_out,
+    wide_mine,
+    head_mine,
+    x_held,
+    out_held,
+    query_held,
+    attn_held,
+    wide_row,
+    head_row,
+    wide_left,
+    head_left,
+    wide_right,
+    head_right,
+    wide_leaving,
+    head_leaving,
+    x_sem,
+    out_sem,
+    query_sem,
+    attn_sem,
+    row_send,
+    row_recv,
+    line_send,
+    left_recv,
+    right_recv,
+):
+    layers, tokens, _ = acts.shape
+    width = wide_out.shape[0] // layers
+    half = head_out.shape[1]
+    size = count * share_rows
+    heads = grad_query.shape[2] // size
+    all_heads = head_out.shape[0] // (layers * share_rows)
+    ins, outs = [wide_mine, head_mine], [wide_out, head_out]
+    from_row, leaving = [wide_row, head_row], [wide_leaving, head_leaving]
+    from_left, from_right = [wide_left, head_left], [wide_right, head_right]
     me, z, y, m = place(count)
     row_mate = {"dp": me + 1 - 2 * y}
     has_left, has_right = z > 0, z < m - 1
-    greet(z, m, [row_mate])
+
+    def order(j):
+        return jnp.where(2 * z < m, m - 1 - j, j)
+
+    for j in range(m):
+        for slot in (order(j) * 2 + 1 - y, order(j) * 2 + y):
+            column_copy(acts, x_held, x_sem, slot, width).start()
+            column_copy(grad_out, out_held, out_sem, slot, width).start()
+    for layer in range(layers):
+        pltpu.make_async_copy(grad_query.at[layer], query_held.at[layer], query_sem.at[layer]).start()
+        pltpu.make_async_copy(attn_out.at[layer], attn_held.at[layer], attn_sem.at[layer]).start()
+
+    def right_side(layer, first, amount):
+        return low[layer, :, first * half : (first + amount) * half]
+
+    def wide_chunk(slot):
+        column_copy(acts, x_held, x_sem, slot, width).wait()
+        column_copy(grad_out, out_held, out_sem, slot, width).wait()
+        for layer in range(layers):
+            grad = product(x_held[slot, layer], right_side(layer, 0, 2), 0) + product(
+                out_held[slot, layer], right_side(layer, 2, 2), 0
+            )
+            wide_mine[slot, layer * width : (layer + 1) * width, :] = (adapter_scale * grad).astype(
+                jnp.bfloat16
+            )
+
+    span = max(1, 16 // share_rows)
+
+    def put_heads(layer, head, grad, amount):
+        grad = adapter_scale * grad
+        for j in range(0, amount, span):
+            start = pl.multiple_of((layer * all_heads + head + j) * share_rows, span * share_rows)
+            for slot in range(count):
+                lows = [(j + i) * size + slot * share_rows for i in range(span)]
+                rows = [grad[low_row : low_row + share_rows] for low_row in lows]
+                rows = rows[0] if span == 1 else jnp.concatenate(rows, axis=0)
+                head_mine[slot, pl.ds(start, span * share_rows), :] = rows.astype(jnp.bfloat16)
 
     def across(p, zz):
         return remote(
@@ -257,26 +541,41 @@
             leaving[p].at[zz], from_right[p].at[zz], line_send.at[p, zz], right_recv.at[p, zz], {"dp": me - 2}
         )
 
-    for k in range(m - 1, 0, -1):
-        for p in range(pieces):
-
-            @pl.when(z + k < m)
+    greet(z, m, [row_mate])
+    for j in range(m):
+        wide_chunk(order(j) * 2 + 1 - y)
+        across(0, order(j)).start()
+
+    group = 2 if heads % 2 == 0 else 1
+    for layer in range(layers):
+        pltpu.make_async_copy(grad_query.at[layer], query_held.at[layer], query_sem.at[layer]).wait()
+        pltpu.make_async_copy(attn_out.at[layer], attn_held.at[layer], attn_sem.at[layer]).wait()
+
+        def step(i, carry):
+            columns = pl.ds(pl.multiple_of(i * group * size, group * size), group * size)
+            grad = product(query_held[layer, :, columns], right_side(layer, 4, 1), 0) + product(
+                attn_held[layer, :, columns], right_side(layer, 5, 1), 0
+            )
+            put_heads(layer, i * group, grad, group)
+            return carry
+
+        lax.fori_loop(0, heads // group, step, 0)
+        kv = product(key_grad[layer], right_side(layer, 6, 1), 0) + product(
+            value_grad[layer], right_side(layer, 7, 1), 0
+        )
+        put_heads(layer, heads, kv, all_heads - heads)
+
+    for j in range(m):
+        across(1, order(j)).start()
+    for j in range(m):
+        wide_chunk(order(j) * 2 + y)
+
+    for p in range(2):
+        for j in range(m):
+            zz = order(j)
+
+            @pl.when(zz > z)
             def _():
-                across(p, z + k).start()
-
-            @pl.when(z - k >= 0)
-            def _():
-                across(p, z - k).start()
-
-    for p in range(pieces):
-        across(p, z).start()
-
-    for k in range(m - 1, 0, -1):
-        for p in range(pieces):
-
-            @pl.when(z + k < m)
-            def _():
-                zz = z + k
                 across(p, zz).wait_recv()
                 near = [ins[p].at[zz * 2 + y], from_row[p].at[zz]]
 
@@ -291,9 +590,8 @@
 
                 right(p, zz).start()
 
-            @pl.when(z - k >= 0)
+            @pl.when(zz < z)
             def _():
-                zz = z - k
                 across(p, zz).wait_recv()
                 near = [ins[p].at[zz * 2 + y], from_row[p].at[zz]]
 
@@ -308,7 +606,7 @@
 
                 left(p, zz).start()
 
-    for p in range(pieces):
+    for p in range(2):
         across(p, z).wait_recv()
         add_rows(outs[p], [ins[p].at[me], from_row[p].at[z]])
 
@@ -334,40 +632,47 @@
                 left(p, zz).wait_send()
 
 
-def scatter_dp(arrays, count, collective_id):
-    pieces, m = len(arrays), count // 2
+def backward(acts, grad_out, grad_query, attn_out, key_grad, value_grad, low, width, all_heads, share_rows, count, collective_id):
+    layers, tokens, _ = acts.shape
+    half, m = low.shape[2] // 8, count // 2
     dma = pltpu.SemaphoreType.DMA
-    slots = [pltpu.VMEM((m,) + a.shape[1:], a.dtype) for a in arrays]
-    vmem = pl.BlockSpec(memory_space=pltpu.VMEM)
+    anywhere, vmem = pl.BlockSpec(memory_space=pl.ANY), pl.BlockSpec(memory_space=pltpu.VMEM)
+    wide = (layers * width, 2 * half)
+    head = (layers * all_heads * share_rows, half)
+    slots = [pltpu.VMEM((m,) + shape, jnp.bfloat16) for shape in (wide, head)]
     return pl.pallas_call(
-        functools.partial(scatter_kernel, count, pieces),
-        out_shape=[jax.ShapeDtypeStruct(a.shape[1:], jnp.float32) for a in arrays],
-        in_specs=[vmem] * pieces,
-        out_specs=[vmem] * pieces,
-        scratch_shapes=slots * 4 + [dma((pieces, m))] * 5,
+        functools.partial(backward_kernel, count, share_rows),
+        out_shape=[jax.ShapeDtypeStruct(shape, jnp.float32) for shape in (wide, head)],
+        in_specs=[anywhere] * 4 + [vmem] * 3,
+        out_specs=[vmem] * 2,
+        scratch_shapes=[pltpu.VMEM((count,) + shape, jnp.bfloat16) for shape in (wide, head)]
+        + [
+            pltpu.VMEM((count, layers, tokens, width), acts.dtype),
+            pltpu.VMEM((count, layers, tokens, width), acts.dtype),
+            pltpu.VMEM(grad_query.shape, grad_query.dtype),
+            pltpu.VMEM(attn_out.shape, attn_out.dtype),
+        ]
+        + slots * 4
+        + [dma((count,)), dma((count,)), dma((layers,)), dma((layers,))]
+        + [dma((2, m))] * 5,
         compiler_params=pltpu.CompilerParams(
-            collective_id=collective_id, has_side_effects=True, vmem_limit_bytes=40 * 2**20
+            collective_id=collective_id, has_side_effects=True, vmem_limit_bytes=48 * 2**20
         ),
-        name="sum_to_owners",
-    )(*arrays)
+        name="gradients_to_owners",
+    )(acts, grad_out, grad_query, attn_out, key_grad, value_grad, low)
 
 
 def merge_kernel(first, heads, away_ref, near_ref, mix, here, there, up, down, out):
     away = away_ref[pl.program_id(1)]
     rank = up.shape[-1]
-    down_part = down[0][:, first : first + rank]
+    down_part = down[0, first : first + rank, :]
 
     def run(base):
         def step(h, carry):
-            mixed_up = jnp.dot(mix[...], up[0, h], preferred_element_type=jnp.float32)
-            product = lax.dot_general(
-                mixed_up.astype(jnp.bfloat16),
-                down_part,
-                (((1,), (1,)), ((), ())),
-                preferred_element_type=jnp.float32,
-            )
-            rows = jnp.dot(mix[...], base[0, h], preferred_element_type=jnp.float32)
-            out[0, h] = (rows + adapter_scale * product).astype(jnp.bfloat16)
+            mixed_up = (adapter_scale * product(mix[...], up[0, 0, h])).astype(jnp.bfloat16)
+            left = jnp.concatenate([mix[...], mixed_up], axis=1)
+            right = jnp.concatenate([base[0, h], down_part], axis=0)
+            out[0, h] = product(left, right).astype(jnp.bfloat16)
             return carry
 
         lax.fori_loop(0, heads, step, 0, unroll=True)
@@ -381,7 +686,7 @@
         run(there)
 
 
-def merge(base_here, base_there, rank_up, rank_down, mix, away, near, first):
+def merge(base_here, base_there, rank_up, rank_down, mix, away, near, first, low_head):
     layers, head_count, size, width = base_here.shape
     slots = away.shape[0]
     per_slot = head_count // slots
@@ -397,6 +702,9 @@
 
     def slot_map(l, g, c, away, near):
         return l, g * steps + c, 0, 0
+
+    def up_map(l, g, c, away, near):
+        return away[g], l, low_head // heads + near[g] * steps + c, 0, 0
 
     block = (1, heads, size, width)
     return pl.pallas_call(
@@ -409,8 +717,8 @@
                 pl.BlockSpec((size, size), lambda l, g, c, away, near: (0, 0)),
                 pl.BlockSpec(block, here_map),
                 pl.BlockSpec(block, there_map),
-                pl.BlockSpec((1, heads, size, rank), slot_map),
-                pl.BlockSpec((1, width, rank_down.shape[-1]), lambda l, g, c, away, near: (l, 0, 0)),
+                pl.BlockSpec((1, 1, heads, size, rank), up_map),
+                pl.BlockSpec((1, rank_down.shape[1], width), lambda l, g, c, away, near: (l, 0, 0)),
             ],
             out_specs=pl.BlockSpec(block, slot_map),
         ),
@@ -456,77 +764,13 @@
 
     wide_bf = wide_params.astype(jnp.bfloat16).reshape(-1, 4 * rank)
     head_bf = jnp.concatenate([head_params, key_value_adapters], axis=1).astype(jnp.bfloat16)
-    wide_all, head_all = gather_dp([wide_bf, head_bf.reshape(-1, 2 * rank)], [], count, False, 0)
-    wide_all = wide_all.reshape(count, layers, wide_rows, 4 * rank)
-    head_all = head_all.reshape(count, layers, all_heads, share_rows, 2 * rank)
-    head_all = head_all.transpose(1, 2, 0, 3, 4).reshape(layers, all_heads, -1, 2 * rank)
-
-    def own_columns(value):
-        split = value.reshape(layers, tokens, count, 2, wide_rows)
-        return lax.dynamic_index_in_dim(split, tensor_pos, 3, keepdims=False).reshape(
-            layers, tokens, count * wide_rows
-        )
-
-    x_own, out_own = own_columns(acts), own_columns(grad_out)
     weight_col = token_weights(seq_lengths, group_ids, rewards, tokens)[:, None]
-    dot = functools.partial(jnp.dot, preferred_element_type=jnp.float32)
-    parts = []
-    for layer in range(layers):
-        wide = wide_all[:, layer].reshape(-1, 4 * rank)
-        flat_head = head_all[layer, :heads].reshape(-1, 2 * rank)
-        flat_kv = head_all[layer, heads:].reshape(-1, 2 * rank)
-        parts.append(
-            jnp.concatenate(
-                [
-                    dot(x_own[layer], wide)[:, : 3 * rank],
-                    dot(out_own[layer], wide)[:, 3 * rank :],
-                    dot(grad_query[layer], flat_head)[:, :rank],
-                    dot(attn_out[layer], flat_head)[:, rank:],
-                    dot(keyvalue_gradient[layer, :, 0], flat_kv)[:, :rank],
-                    dot(keyvalue_gradient[layer, :, 1], flat_kv)[:, rank:],
-                ],
-                axis=1,
-            )
-        )
-    part = jnp.stack(parts)
-    low = (weight_col * (part + swap_core(part))).astype(jnp.bfloat16)
-    wide_chunks, head_chunks = [], []
-    for layer in range(layers):
-        hidden = low[layer, :, : 3 * rank]
-        gate_output = low[layer, :, 3 * rank : 4 * rank]
-        gate_query = low[layer, :, 4 * rank : 5 * rank]
-        hidden_output = low[layer, :, 5 * rank : 6 * rank]
-        gate_kv = low[layer, :, 6 * rank :]
-        none = jnp.zeros((tokens, rank), jnp.bfloat16)
-        wide_grad = contracted_rows(
-            x_own[layer], jnp.concatenate([gate_query, gate_kv, none], axis=1)
-        ) + contracted_rows(
-            out_own[layer], jnp.concatenate([none, none, none, hidden_output], axis=1)
-        )
-        head_grad = contracted_rows(
-            grad_query[layer], jnp.concatenate([hidden[:, :rank], none], axis=1)
-        ) + contracted_rows(attn_out[layer], jnp.concatenate([none, gate_output], axis=1))
-        kv_grad = contracted_rows(
-            keyvalue_gradient[layer, :, 0],
-            jnp.concatenate([hidden[:, rank : 2 * rank], none], axis=1),
-        ) + contracted_rows(
-            keyvalue_gradient[layer, :, 1],
-            jnp.concatenate([none, hidden[:, 2 * rank :]], axis=1),
-        )
-        wide_chunks.append((adapter_scale * wide_grad).astype(jnp.bfloat16))
-        head_chunks.append(
-            jnp.concatenate(
-                [
-                    (adapter_scale * grad).astype(jnp.bfloat16).reshape(-1, count, share_rows, 2 * rank)
-                    for grad in (head_grad, kv_grad)
-                ]
-            ).transpose(1, 0, 2, 3)
-        )
-    wide_send = jnp.stack(
-        [chunk.reshape(count, wide_rows, 4 * rank) for chunk in wide_chunks], axis=1
-    ).reshape(count, -1, 4 * rank)
-    head_send = jnp.stack(head_chunks, axis=1).reshape(count, -1, 2 * rank)
-    wide_sum, head_sum = scatter_dp([wide_send, head_send], count, 1)
+    key_grad, value_grad = keyvalue_gradient[:, :, 0], keyvalue_gradient[:, :, 1]
+    rows = (acts, grad_out, grad_query, attn_out, key_grad, value_grad)
+    low = forward(
+        wide_bf, head_bf.reshape(-1, 2 * rank), *rows, weight_col, count, share_rows, 0
+    )
+    wide_sum, head_sum = backward(*rows, low, wide_rows, all_heads, share_rows, count, 1)
     wide_grad = wide_sum.reshape(wide_params.shape)
     head_sum = head_sum.reshape(layers, all_heads, share_rows, 2 * rank)
     new_wide, new_wide_moments = adamw(wide_params, wide_moments, wide_grad)
@@ -542,7 +786,7 @@
     first = tensor_pos == 0
     rank_down = jnp.concatenate(
         [jnp.where(first, down_own, down_there), jnp.where(first, down_there, down_own)], axis=1
-    )
+    ).transpose(0, 2, 1)
 
     slot_groups = kv_heads
     group_slots = tensor_pos * slot_groups + jnp.arange(slot_groups, dtype=jnp.int32)
@@ -551,31 +795,15 @@
     near = (source_groups % slot_groups).astype(jnp.int32)
 
     both = jnp.stack([up_here, up_there]).reshape(2, count, layers, all_heads, share_rows, rank)
-
-    def picked(low_head, amount):
-        grouped = both[:, :, :, low_head : low_head + amount].reshape(
-            2, count, layers, slot_groups, amount // slot_groups, share_rows, rank
-        )
-        rows = [
-            lax.dynamic_index_in_dim(
-                lax.dynamic_index_in_dim(grouped, away[slot], 0, keepdims=False),
-                near[slot],
-                2,
-                keepdims=False,
-            )
-            for slot in range(slot_groups)
-        ]
-        stacked = jnp.stack(rows, axis=2)
-        return stacked.transpose(1, 2, 3, 0, 4, 5).reshape(layers, amount, -1, rank)
-
+    both = both.transpose(0, 2, 3, 1, 4, 5).reshape(2, layers, all_heads, -1, rank)
     mix = (rotary_rows[:, None] == jnp.arange(rotary_rows.shape[0], dtype=jnp.int32)[None, :]).astype(
         jnp.bfloat16
     )
     merged_query = merge(
-        base_query, base_there, picked(0, heads), rank_down, mix, away, near, 0
+        base_query, base_there, both, rank_down, mix, away, near, 0, 0
     )
     merged_key = merge(
-        frozen_key_rows, frozen_there, picked(heads, kv_heads), rank_down, mix, away, near, rank
+        frozen_key_rows, frozen_there, both, rank_down, mix, away, near, rank, heads
     )
     return (
         new_wide,

time: 252 us -> 208 us (0.83)
  matrix products: 25.2 us -> 0 us
  local copies, waits for them, and re-layouts: 52.1 us -> 29.7 us
  Pallas kernels: 146 us -> 160 us
  between operations: 9.14 us -> 0.96 us
    pallas_call x1 -> x2, Pallas kernels: 50.6 us -> 119 us  [the longest x1 59.8 us: backward(): pl.pallas_call(functools.partial(backward_kernel, count, share_rows), out...]
    pallas_call x2 -> x1, Pallas kernels: 74 us -> 22.7 us  [gather_dp(): pl.pallas_call(functools.partial(gather_kernel, count, pieces, share, swa...]
    dot_general x24 -> x0, matrix products: 25.2 us -> none  [the longest x12 13.5 us: contracted_rows(): lax.dot_general(left, right, (((0,), (0,)), ((), ())), preferred_element_...]
    unnamed x123 -> x35, local copies, waits for them, and re-layouts: 21.2 us -> 11.3 us
    convert_element_type x4 -> x0, local copies, waits for them, and re-layouts: 6.19 us -> none  [body(): (adapter_scale * grad).astype(jnp.bfloat16)]
    slice x11 -> x2, local copies, waits for them, and re-layouts: 8.61 us -> 3.53 us  [the longest x1 2.25 us: body(): keyvalue_gradient[:, :, 1]]
    pallas_call x2, Pallas kernels: 21.2 us -> 18 us  [merge(): pl.pallas_call(functools.partial(merge_kernel, first, heads), out_shape=j...]
    another operation x9 -> x3, other arithmetic: 5.41 us -> 4.51 us  [the longest x1 2.66 us: body(): jnp.stack([up_here, up_there])]
  transfers between devices with their start and end apart: 3 -> 2, of which waited for: 0 -> 0; matrix products, arithmetic and copies ran while one was open for 20% -> 19% of each run, Pallas kernels for 30% -> 70%
where the time goes in v2:
time: 208 us; the launch traced here: 207 us
  Pallas kernels  160 us (77%)
  local copies, waits for them, and re-layouts  29.7 us (14%)
  other arithmetic  16.3 us (8%)
    pallas_call x1, Pallas kernels, backward(): pl.pallas_call(functools.partial(backward_kernel, count, share_rows), out...  59.8 us
    pallas_call x1, Pallas kernels, forward(): pl.pallas_call(functools.partial(forward_kernel, count, share_rows), out_...  59.4 us
    pallas_call x1, Pallas kernels, gather_dp(): pl.pallas_call(functools.partial(gather_kernel, count, pieces, share, swa...  22.7 us
    pallas_call x2, Pallas kernels, merge(): pl.pallas_call(functools.partial(merge_kernel, first, heads), out_shape=j...  18 us
    unnamed x35, local copies, waits for them, and re-layouts  11.3 us
    another operation x3, local copies, waits for them, and re-layouts, body(): jnp.stack([up_here, up_there])  10.2 us
    another operation x5, other arithmetic, adamw(): jnp.stack([first_moment, second_moment])  4.39 us
  transfers between devices with their start and end apart: 2, of which 0 were waited for; matrix products, arithmetic and copies ran while one was open for 19% of the time, Pallas kernels for 70%

profile of v2, /device:TPU:0, one launch (start us, length us, event | category | flops | bytes accessed | tf_op | source)
XLA Modules:
  0.0 207.3 jit_solution(413770618286912666)
XLA Ops:
  1.2 2.0 copy.65
  3.3 1.1 convert_element_type.35
  4.4 0.8 convert.18
  5.1 1.1 convert.17
  6.2 0.8 reduce_window_sum.11
  7.0 0.9 fusion.17
  8.0 0.7 subtract_bitcast_fusion
  8.6 0.7 fusion.20
  9.6 2.3 %fusion.22 = (bf16[2,256,1,256]{3,2,1,0:T(2,128)(2,1)S(1)}, bf16[2,256,1,256]{3,2,1,0:T(2,128)(2,1)S(1)}) fusion(bf16[2,256,2,256]{3,2,1,0:T(2,128)(2,1)} %param.20), kind=kLoop, calls=%fused_computation.66 | loop fusion | bytes 1048576 | tf_op jit(solution)/shard_map/slice | solution.py:768
  12.1 59.4 %gather_and_low_products.1.low = bf16[2,256,1024]{2,1,0:T(8,128)(2,1)S(1)} custom-call(bf16[512,256]{1,0:T(8,128)(2,1)S(1)} %bitcast.83, bf16[1088,128]{1,0:T(8,128)(2,1)S(1)} %bitcast.82, bf16[2,256,4096]{2,1,0:T(8,128)(2,1)S(1)} %copy-done.3, bf16[2,256,4096]{2,1,0:T(8,128)(2,1)} %grad_out.3, bf16[2,256,4096]{2,1,0:T(8,128)(2,1)} %grad_query.3, ...), custom_call_target="tpu_custom_call" | custom-call | tf_op jit(solution)/shard_map/gather_and_low_products/pallas_call | solution.py:394
  71.4 59.8 %gradients_to_owners.1 = (f32[512,256]{1,0:T(8,128)S(1)}, f32[1088,128]{1,0:T(8,128)S(1)}) custom-call(bf16[2,256,4096]{2,1,0:T(8,128)(2,1)} %acts.3, bf16[2,256,4096]{2,1,0:T(8,128)(2,1)} %grad_out.3, bf16[2,256,4096]{2,1,0:T(8,128)(2,1)} %grad_query.3, bf16[2,256,4096]{2,1,0:T(8,128)(2,1)} %attn_out.3, ...), custom_call_target="tpu_custom_call" | custom-call | tf_op jit(solution)/shard_map/gradients_to_owners/pallas_call | solution.py:643
  131.2 1.0 copy.60
  132.2 1.3 fusion.21
  133.9 1.6 multiply_subtract_fusion.1
  135.5 1.0 copy.74
  136.5 1.0 copy.66
  137.5 1.2 multiply_add_fusion
  138.9 1.3 copy.75
  140.3 2.6 %fusion.9 = (f32[1,2,32,16,128]{4,3,2,1,0:T(8,128)}, f32[1,2,32,16,128]{4,3,2,1,0:T(8,128)}, f32[2,32,16,128]{3,2,1,0:T(8,128)S(1)}) fusion(f32[2,34,16,128]{3,2,1,0:T(8,128)S(1)} %bitcast.85, f32[2,2,32,16,128]{4,3,2,1,0:T(8,128)} %param.29, f32[2,32,16,128]{3,2,1,0:T(8,128)S(1)} %copy-done.6), kind=kLoop, calls=%fused_computation.30 | loop fusion | flops 1966080 | bytes 3670016 | tf_op jit(solution)/shard_map/stack | solution.py:47
  142.9 0.8 copy-done.9
  143.8 0.8 convert_element_type.41.refs_0_
  144.6 0.8 copy.69
  145.4 22.7 %gather_pieces.1 = (bf16[8,544,128]{2,1,0:T(8,128)(2,1)}, bf16[8,544,128]{2,1,0:T(8,128)(2,1)}, bf16[512,128]{1,0:T(8,128)(2,1)}) custom-call(bf16[544,128]{1,0:T(8,128)(2,1)} %convert_element_type.41.refs_0_, bf16[512,128]{1,0:T(8,128)(2,1)} %bitcast.86), custom_call_target="tpu_custom_call" | custom-call | tf_op jit(solution)/shard_map/gather_pieces/pallas_call | solution.py:224
  168.1 2.9 %stack.40 = bf16[1,8,2,34,16,64]{5,4,3,2,1,0:T(8,128)(2,1)S(1)} reshape(bf16[8,544,128]{2,1,0:T(8,128)(2,1)} %get-tuple-element.16) | data formatting | bytes 2228224 | tf_op jit(solution)/shard_map/stack | solution.py:797
  171.0 3.9 %stack.39 = bf16[1,8,2,34,16,64]{5,4,3,2,1,0:T(8,128)(2,1)} reshape(bf16[8,544,128]{2,1,0:T(8,128)(2,1)} %get-tuple-element.15) | data formatting | bytes 2228224 | tf_op jit(solution)/shard_map/stack | solution.py:797
  174.9 2.7 %pad_maximum_fusion = bf16[2,8,2,34,16,64]{5,4,3,2,1,0:T(8,128)(2,1)S(1)} fusion(bf16[1,8,2,34,16,64]{5,4,3,2,1,0:T(8,128)(2,1)S(1)} %stack.40, bf16[1,8,2,34,16,64]{5,4,3,2,1,0:T(8,128)(2,1)} %stack.39), kind=kLoop, calls=%fused_computation.1 | loop fusion | flops 1114112 | bytes 4456448 | tf_op jit(solution)/shard_map/stack | solution.py:797
  177.6 3.4 %copy.76 = bf16[2,8,2,34,16,64]{5,4,1,3,2,0:T(8,128)(2,1)} copy(bf16[2,8,2,34,16,64]{5,4,3,2,1,0:T(8,128)(2,1)S(1)} %pad_maximum_fusion) | data formatting | bytes 4456448 | tf_op jit(solution)/shard_map/stack | solution.py:797
  181.9 1.0 pad_maximum_fusion.2
  183.7 2.3 %copy-done.1 = bf16[2,8,2,34,16,64]{5,4,1,3,2,0:T(8,128)(2,1)S(1)} copy-done((bf16[2,8,2,34,16,64]{5,4,1,3,2,0:T(8,128)(2,1)S(1)}, bf16[2,8,2,34,16,64]{5,4,1,3,2,0:T(8,128)(2,1)}, u32[]{:S(2)}) %copy-start.1) | copy-done | bytes 2228248
  186.0 2.9 %merged_rows.3 = bf16[2,2,128,512]{3,2,1,0:T(8,128)(2,1)} custom-call(s32[2]{0:T(128)S(1)} %compare_convert_fusion.1.away_ref, s32[2]{0:T(128)S(1)} %get-tuple-element.44.near_ref, bf16[128,128]{1,0:T(8,128)(2,1)S(1)} %fusion.11.mix, bf16[2,2,128,512]{3,2,1,0:T(8,128)(2,1)S(1)} %copy-done.5, bf16[2,2,128,512]{3,2,1,0:T(8,128)(2,1)S(1)} %collective-permute-done.1.there, ...), custom_call_target="tpu_custom_call" | custom-call | tf_op jit(solution)/shard_map/merged_rows/pallas_call | solution.py:710
  188.9 3.4 %copy-done.4 = bf16[2,32,128,512]{3,2,1,0:T(8,128)(2,1)S(1)} copy-done((bf16[2,32,128,512]{3,2,1,0:T(8,128)(2,1)S(1)}, bf16[2,32,128,512]{3,2,1,0:T(8,128)(2,1)}, u32[]{:S(2)}) %copy-start.4) | copy-done | bytes 8388632
  192.2 15.1 %merged_rows.2 = bf16[2,32,128,512]{3,2,1,0:T(8,128)(2,1)} custom-call(s32[2]{0:T(128)S(1)} %compare_convert_fusion.1.away_ref, s32[2]{0:T(128)S(1)} %get-tuple-element.44.near_ref, bf16[128,128]{1,0:T(8,128)(2,1)S(1)} %fusion.11.mix, bf16[2,32,128,512]{3,2,1,0:T(8,128)(2,1)S(1)} %copy-done.4, bf16[2,32,128,512]{3,2,1,0:T(8,128)(2,1)} %collective-permute-done.there, ...), custom_call_target="tpu_custom_call" | custom-call | tf_op jit(solution)/shard_map/merged_rows/pallas_call | solution.py:710
  (53 shorter events, 3.3 us)
Async XLA Ops:
  0.6 180.5 %copy-start = (s32[4]{0:T(128)S(1)}, s32[4]{0:T(128)}, u32[]{:S(2)}) copy-start(s32[4]{0:T(128)} %param.35) | copy-start | bytes 52
  0.6 188.2 %collective-permute-start = (bf16[2,32,128,512]{3,2,1,0:T(8,128)(2,1)}, bf16[2,32,128,512]{3,2,1,0:T(8,128)(2,1)}, u32[]{:S(2)}, u32[]{:S(2)}) collective-permute-start(bf16[2,32,128,512]{3,2,1,0:T(8,128)(2,1)} %here.2), channel_id=1, source_target_pairs={{0,1},{1,0},{2,3},{3,2},{4,5},{5,4},{6,7},{7,6},{8,9},{9,8},{10,11... | collective-permute-start | bytes 25165832 | tf_op jit(solution)/shard_map/ppermute | solution.py:731
  1.2 182.5 %collective-permute-start.1 = (bf16[2,2,128,512]{3,2,1,0:T(8,128)(2,1)}, bf16[2,2,128,512]{3,2,1,0:T(8,128)(2,1)S(1)}, u32[]{:S(2)}, u32[]{:S(2)}) collective-permute-start(bf16[2,2,128,512]{3,2,1,0:T(8,128)(2,1)} %here.3), channel_id=1, source_target_pairs={{0,1},{1,0},{2,3},{3,2},{4,5},{5,4},{6,7},{7,6},{8,9},{9,8},{10,11... | collective-permute-start | bytes 1572872 | tf_op jit(solution)/shard_map/ppermute | solution.py:731
  9.6 2.5 %copy-start.3 = (bf16[2,256,4096]{2,1,0:T(8,128)(2,1)S(1)}, bf16[2,256,4096]{2,1,0:T(8,128)(2,1)}, u32[]{:S(2)}) copy-start(bf16[2,256,4096]{2,1,0:T(8,128)(2,1)} %acts.3) | copy-start | bytes 12582916
  136.5 3.7 %copy-start.10 = (f32[2,2,16,128]{3,2,1,0:T(8,128)S(1)}, f32[2,2,16,128]{3,2,1,0:T(8,128)}, u32[]{:S(2)}) copy-start(f32[2,2,16,128]{3,2,1,0:T(8,128)} %param.30) | copy-start | bytes 98308
  136.5 3.7 %copy-start.13 = (f32[2,2,2,16,128]{4,3,2,1,0:T(8,128)S(1)}, f32[2,2,2,16,128]{4,3,2,1,0:T(8,128)}, u32[]{:S(2)}) copy-start(f32[2,2,2,16,128]{4,3,2,1,0:T(8,128)} %param.31) | copy-start | bytes 196612
  138.8 1.5 copy-start.6
  140.2 30.7 %copy-start.12 = (f32[2,2,16,128]{3,2,1,0:T(8,128)}, f32[2,2,16,128]{3,2,1,0:T(8,128)S(1)}, u32[]{:S(2)}) copy-start(f32[2,2,16,128]{3,2,1,0:T(8,128)S(1)} %get-tuple-element.53) | copy-start | bytes 98308
  142.9 0.8 copy-start.9
  177.5 3.5 %copy-start.11 = (bf16[512,128]{1,0:T(8,128)(2,1)S(1)}, bf16[512,128]{1,0:T(8,128)(2,1)}, u32[]{:S(2)}) copy-start(bf16[512,128]{1,0:T(8,128)(2,1)} %get-tuple-element.17) | copy-start | bytes 393220
  177.5 4.3 %copy-start.7 = (f32[1,2,32,16,128]{4,3,2,1,0:T(8,128)S(1)}, f32[1,2,32,16,128]{4,3,2,1,0:T(8,128)}, u32[]{:S(2)}) copy-start(f32[1,2,32,16,128]{4,3,2,1,0:T(8,128)} %get-tuple-element.46) | copy-start | bytes 1572868
  177.6 4.3 %copy-start.8 = (f32[1,2,32,16,128]{4,3,2,1,0:T(8,128)S(1)}, f32[1,2,32,16,128]{4,3,2,1,0:T(8,128)}, u32[]{:S(2)}) copy-start(f32[1,2,32,16,128]{4,3,2,1,0:T(8,128)} %get-tuple-element.47) | copy-start | bytes 1572868
  177.6 6.0 %copy-start.14 = (s32[128]{0:T(128)S(1)}, s32[128]{0:T(128)}, u32[]{:S(2)}) copy-start(s32[128]{0:T(128)} %param.34) | copy-start | bytes 1540
  181.0 2.7 %copy-start.5 = (bf16[2,2,128,512]{3,2,1,0:T(8,128)(2,1)S(1)}, bf16[2,2,128,512]{3,2,1,0:T(8,128)(2,1)}, u32[]{:S(2)}) copy-start(bf16[2,2,128,512]{3,2,1,0:T(8,128)(2,1)} %here.3) | copy-start | bytes 1572868
  183.7 2.3 %copy-start.1 = (bf16[2,8,2,34,16,64]{5,4,1,3,2,0:T(8,128)(2,1)S(1)}, bf16[2,8,2,34,16,64]{5,4,1,3,2,0:T(8,128)(2,1)}, u32[]{:S(2)}) copy-start(bf16[2,8,2,34,16,64]{5,4,1,3,2,0:T(8,128)(2,1)} %copy.76) | copy-start | bytes 6684676
  186.0 2.9 %copy-start.2 = (bf16[2,8,2,34,16,64]{5,4,1,3,2,0:T(8,128)(2,1)S(1)}, bf16[2,8,2,34,16,64]{5,4,1,3,2,0:T(8,128)(2,1)}, u32[]{:S(2)}) copy-start(bf16[2,8,2,34,16,64]{5,4,1,3,2,0:T(8,128)(2,1)} %copy.76) | copy-start | bytes 6684676
  188.8 3.4 %copy-start.4 = (bf16[2,32,128,512]{3,2,1,0:T(8,128)(2,1)S(1)}, bf16[2,32,128,512]{3,2,1,0:T(8,128)(2,1)}, u32[]{:S(2)}) copy-start(bf16[2,32,128,512]{3,2,1,0:T(8,128)(2,1)} %here.2) | copy-start | bytes 25165828

commit v3 on v2

--- a/solution.py
+++ b/solution.py
@@ -662,37 +662,41 @@
     )(acts, grad_out, grad_query, attn_out, key_grad, value_grad, low)
 
 
-def merge_kernel(first, heads, away_ref, near_ref, mix, here, there, up, down, out):
+def merge_kernel(heads, away_ref, near_ref, mix, here, there, up_here, up_there, down, out):
     away = away_ref[pl.program_id(1)]
-    rank = up.shape[-1]
-    down_part = down[0, first : first + rank, :]
-
-    def run(base):
-        def step(h, carry):
-            mixed_up = (adapter_scale * product(mix[...], up[0, 0, h])).astype(jnp.bfloat16)
+    count, share_rows = up_here.shape[0], up_here.shape[1] // heads
+
+    def run(base, up):
+        for h in range(heads):
+            if share_rows % 16 == 0:
+                rows = [up[slot, h * share_rows : (h + 1) * share_rows, :] for slot in range(count)]
+            else:
+                rows = [
+                    up[slot].astype(jnp.float32)[h * share_rows : (h + 1) * share_rows]
+                    for slot in range(count)
+                ]
+            ups = jnp.concatenate(rows, axis=0).astype(jnp.bfloat16)
+            mixed_up = (adapter_scale * product(mix[...], ups)).astype(jnp.bfloat16)
             left = jnp.concatenate([mix[...], mixed_up], axis=1)
-            right = jnp.concatenate([base[0, h], down_part], axis=0)
+            right = jnp.concatenate([base[0, h], down[0]], axis=0)
             out[0, h] = product(left, right).astype(jnp.bfloat16)
-            return carry
-
-        lax.fori_loop(0, heads, step, 0, unroll=True)
 
     @pl.when(away == 0)
     def _():
-        run(here)
+        run(here, up_here)
 
     @pl.when(away != 0)
     def _():
-        run(there)
-
-
-def merge(base_here, base_there, rank_up, rank_down, mix, away, near, first, low_head):
+        run(there, up_there)
+
+
+def merge(base_here, base_there, up_here, up_there, down, mix, away, near, low_head, share_rows):
     layers, head_count, size, width = base_here.shape
+    count, _, ranks = up_here.shape
     slots = away.shape[0]
     per_slot = head_count // slots
     heads = min(8, per_slot)
     steps = per_slot // heads
-    rank = rank_up.shape[-1]
 
     def here_map(l, g, c, away, near):
         return jnp.where(away[g] == 0, l, 0), jnp.where(away[g] == 0, near[g] * steps + c, 0), 0, 0
@@ -704,11 +708,12 @@
         return l, g * steps + c, 0, 0
 
     def up_map(l, g, c, away, near):
-        return away[g], l, low_head // heads + near[g] * steps + c, 0, 0
+        return 0, low_head // heads + near[g] * steps + c, 0
 
     block = (1, heads, size, width)
+    up_block = (count, heads * share_rows, ranks)
     return pl.pallas_call(
-        functools.partial(merge_kernel, first, heads),
+        functools.partial(merge_kernel, heads),
         out_shape=jax.ShapeDtypeStruct(base_here.shape, base_here.dtype),
         grid_spec=pltpu.PrefetchScalarGridSpec(
             num_scalar_prefetch=2,
@@ -717,14 +722,15 @@
                 pl.BlockSpec((size, size), lambda l, g, c, away, near: (0, 0)),
                 pl.BlockSpec(block, here_map),
                 pl.BlockSpec(block, there_map),
-                pl.BlockSpec((1, 1, heads, size, rank), up_map),
-                pl.BlockSpec((1, rank_down.shape[1], width), lambda l, g, c, away, near: (l, 0, 0)),
+                pl.BlockSpec(up_block, up_map),
+                pl.BlockSpec(up_block, up_map),
+                pl.BlockSpec((1,) + down.shape[1:], lambda l, g, c, away, near: (l, 0, 0)),
             ],
             out_specs=pl.BlockSpec(block, slot_map),
         ),
         compiler_params=pltpu.CompilerParams(vmem_limit_bytes=40 * 2**20),
         name="merged_rows",
-    )(away, near, mix, base_here, base_there, rank_up, rank_down)
+    )(away, near, mix, base_here, base_there, up_here, up_there, down)
 
 
 def swap_core(value):
@@ -780,7 +786,7 @@
     up_own = jnp.concatenate([new_head[..., :rank], new_kv[..., :rank]], axis=1).astype(jnp.bfloat16)
     down_own = new_wide[..., : 2 * rank].astype(jnp.bfloat16)
     up_here, up_there, down_there = gather_dp(
-        [up_own.reshape(-1, 2 * rank)], [down_own.reshape(-1, 2 * rank)], count, True, 2
+        [jnp.concatenate(list(up_own), axis=-1).reshape(-1, layers * rank)], [down_own.reshape(-1, 2 * rank)], count, True, 2
     )
     down_there = down_there.reshape(down_own.shape)
     first = tensor_pos == 0
@@ -794,16 +800,29 @@
     away = (source_groups // slot_groups != tensor_pos).astype(jnp.int32)
     near = (source_groups % slot_groups).astype(jnp.int32)
 
-    both = jnp.stack([up_here, up_there]).reshape(2, count, layers, all_heads, share_rows, rank)
-    both = both.transpose(0, 2, 3, 1, 4, 5).reshape(2, layers, all_heads, -1, rank)
+    same_layer = jnp.eye(layers, dtype=jnp.bfloat16)[:, :, None, None]
+
+    def own_layer(part):
+        return (same_layer * part[:, None]).reshape(layers, layers * rank, -1)
+
+    down_query, down_key = own_layer(rank_down[:, :rank]), own_layer(rank_down[:, rank:])
     mix = (rotary_rows[:, None] == jnp.arange(rotary_rows.shape[0], dtype=jnp.int32)[None, :]).astype(
         jnp.bfloat16
     )
     merged_query = merge(
-        base_query, base_there, both, rank_down, mix, away, near, 0, 0
+        base_query, base_there, up_here, up_there, down_query, mix, away, near, 0, share_rows
     )
     merged_key = merge(
-        frozen_key_rows, frozen_there, both, rank_down, mix, away, near, rank, heads
+        frozen_key_rows,
+        frozen_there,
+        up_here,
+        up_there,
+        down_key,
+        mix,
+        away,
+        near,
+        heads,
+        share_rows,
     )
     return (
         new_wide,

time: 208 us -> 190 us (0.913)
  local copies, waits for them, and re-layouts: 29.7 us -> 8.42 us
    another operation x3 -> x0, local copies, waits for them, and re-layouts: 10.2 us -> none  [body(): jnp.stack([up_here, up_there])]
    unnamed x35 -> x36, local copies, waits for them, and re-layouts: 11.3 us -> 3.48 us
    pallas_call x2, Pallas kernels: 18 us -> 20.4 us  [merge(): pl.pallas_call(functools.partial(merge_kernel, heads), out_shape=jax.Shap...]
    another operation x3 -> x2, other arithmetic: 4.51 us -> 2.17 us  [the longest x1 2.66 us: body(): jnp.stack([up_here, up_there])]
    reshape x3 -> x0, local copies, waits for them, and re-layouts: 2.11 us -> none  [the longest x2 1.99 us: body(): wide_grad = wide_sum.reshape(wide_params.shape)]
  transfers between devices with their start and end apart: 2 -> 2, of which waited for: 0 -> 0; matrix products, arithmetic and copies ran while one was open for 19% -> 12% of each run, Pallas kernels for 70% -> 77%
where the time goes in v3:
time: 190 us; the launch traced here: 189 us
  Pallas kernels  162 us (85%)
  other arithmetic  17 us (9%)
  local copies, waits for them, and re-layouts  8.42 us (4%)
    pallas_call x1, Pallas kernels, backward(): pl.pallas_call(functools.partial(backward_kernel, count, share_rows), out...  59.6 us
    pallas_call x1, Pallas kernels, forward(): pl.pallas_call(functools.partial(forward_kernel, count, share_rows), out_...  59.4 us
    pallas_call x1, Pallas kernels, gather_dp(): pl.pallas_call(functools.partial(gather_kernel, count, pieces, share, swa...  22.8 us
    pallas_call x2, Pallas kernels, merge(): pl.pallas_call(functools.partial(merge_kernel, heads), out_shape=jax.Shap...  20.4 us
    another operation x5, other arithmetic, adamw(): jnp.stack([first_moment, second_moment])  6.04 us
  transfers between devices with their start and end apart: 2, of which 0 were waited for; matrix products, arithmetic and copies ran while one was open for 12% of the time, Pallas kernels for 77%

profile of v3, /device:TPU:0, one launch (start us, length us, event | category | flops | bytes accessed | tf_op | source)
XLA Modules:
  0.0 189.2 jit_solution(204007883410405149)
XLA Ops:
  0.6 0.5 collective-permute-start
  1.2 0.8 reduce_window_sum.11
  2.1 0.9 fusion.18
  3.0 0.7 subtract_bitcast_fusion
  3.7 0.7 fusion.21
  4.5 0.1 copy.37.weights
  4.6 1.2 convert.17
  5.8 0.9 convert.18
  6.8 1.1 convert_element_type.40
  7.9 2.2 %fusion.22 = (bf16[2,256,1,256]{3,2,1,0:T(2,128)(2,1)S(1)}, bf16[2,256,1,256]{3,2,1,0:T(2,128)(2,1)S(1)}) fusion(bf16[2,256,2,256]{3,2,1,0:T(2,128)(2,1)} %param.20), kind=kLoop, calls=%fused_computation.73 | loop fusion | bytes 1048576 | tf_op jit(solution)/shard_map/slice | solution.py:774
  10.2 59.4 %gather_and_low_products.1.low = bf16[2,256,1024]{2,1,0:T(8,128)(2,1)S(1)} custom-call(bf16[512,256]{1,0:T(8,128)(2,1)S(1)} %bitcast.82, bf16[1088,128]{1,0:T(8,128)(2,1)S(1)} %bitcast.81, bf16[2,256,4096]{2,1,0:T(8,128)(2,1)S(1)} %copy-done.1, bf16[2,256,4096]{2,1,0:T(8,128)(2,1)} %grad_out.3, bf16[2,256,4096]{2,1,0:T(8,128)(2,1)} %grad_query.3, ...), custom_call_target="tpu_custom_call" | custom-call | tf_op jit(solution)/shard_map/gather_and_low_products/pallas_call | solution.py:394
  69.7 59.6 %gradients_to_owners.1 = (f32[512,256]{1,0:T(8,128)S(1)}, f32[1088,128]{1,0:T(8,128)S(1)}) custom-call(bf16[2,256,4096]{2,1,0:T(8,128)(2,1)} %acts.3, bf16[2,256,4096]{2,1,0:T(8,128)(2,1)} %grad_out.3, bf16[2,256,4096]{2,1,0:T(8,128)(2,1)} %grad_query.3, bf16[2,256,4096]{2,1,0:T(8,128)(2,1)} %attn_out.3, ...), custom_call_target="tpu_custom_call" | custom-call | tf_op jit(solution)/shard_map/gradients_to_owners/pallas_call | solution.py:643
  129.3 1.4 fusion.10
  130.7 0.8 fusion.15
  131.5 0.4 multiply_subtract_fusion.1
  131.9 0.7 slice.126
  132.7 0.8 pad_maximum_fusion.4.refs_0_
  133.5 22.8 %gather_pieces.1 = (bf16[8,544,128]{2,1,0:T(8,128)(2,1)}, bf16[8,544,128]{2,1,0:T(8,128)(2,1)}, bf16[512,128]{1,0:T(8,128)(2,1)}) custom-call(bf16[544,128]{1,0:T(8,128)(2,1)} %pad_maximum_fusion.4.refs_0_, bf16[512,128]{1,0:T(8,128)(2,1)} %bitcast.87), custom_call_target="tpu_custom_call" | custom-call | tf_op jit(solution)/shard_map/gather_pieces/pallas_call | solution.py:224
  156.3 0.9 broadcast_select_fusion.1
  157.3 0.1 fusion.23
  157.4 0.1 copy.38
  157.6 0.1 copy.39
  157.9 0.6 mul.262
  158.5 0.6 gather_fusion
  159.1 0.8 bitcast_multiply_fusion
  159.9 2.3 %pad_maximum_fusion.1 = f32[2,2,32,16,128]{4,3,2,1,0:T(8,128)} fusion(f32[1,2,32,16,128]{4,3,2,1,0:T(8,128)} %get-tuple-element.23, f32[1,2,32,16,128]{4,3,2,1,0:T(8,128)} %get-tuple-element.22), kind=kLoop, calls=%fused_computation.2 | loop fusion | flops 262144 | bytes 2097152 | tf_op jit(solution)/shard_map/stack | solution.py:47
  162.2 1.4 multiply_add_fusion
  163.5 1.0 pad_maximum_fusion
  164.6 0.6 pad_maximum_fusion.5
  165.4 4.3 %merged_rows.3 = bf16[2,2,128,512]{3,2,1,0:T(8,128)(2,1)} custom-call(s32[2]{0:T(128)S(1)} %compare_convert_fusion.2.away_ref, s32[2]{0:T(128)S(1)} %get-tuple-element.20.near_ref, bf16[128,128]{1,0:T(8,128)(2,1)S(1)} %fusion.12.mix, bf16[2,2,128,512]{3,2,1,0:T(8,128)(2,1)S(1)} %copy-done.5, bf16[2,2,128,512]{3,2,1,0:T(8,128)(2,1)} %collective-permute-done.1.there, ...), custom_call_target="tpu_custom_call" | custom-call | tf_op jit(solution)/shard_map/merged_rows/pallas_call | solution.py:715
  169.7 3.4 %copy-done.2 = bf16[2,32,128,512]{3,2,1,0:T(8,128)(2,1)S(1)} copy-done((bf16[2,32,128,512]{3,2,1,0:T(8,128)(2,1)S(1)}, bf16[2,32,128,512]{3,2,1,0:T(8,128)(2,1)}, u32[]{:S(2)}) %copy-start.2) | copy-done | bytes 8388632
  173.1 16.1 %merged_rows.2 = bf16[2,32,128,512]{3,2,1,0:T(8,128)(2,1)} custom-call(s32[2]{0:T(128)S(1)} %compare_convert_fusion.2.away_ref, s32[2]{0:T(128)S(1)} %get-tuple-element.20.near_ref, bf16[128,128]{1,0:T(8,128)(2,1)S(1)} %fusion.12.mix, bf16[2,32,128,512]{3,2,1,0:T(8,128)(2,1)S(1)} %copy-done.2, bf16[2,32,128,512]{3,2,1,0:T(8,128)(2,1)} %collective-permute-done.there, ...), custom_call_target="tpu_custom_call" | custom-call | tf_op jit(solution)/shard_map/merged_rows/pallas_call | solution.py:715
  (52 shorter events, 0.7 us)
Async XLA Ops:
  0.6 157.8 %copy-start = (s32[4]{0:T(128)S(1)}, s32[4]{0:T(128)}, u32[]{:S(2)}) copy-start(s32[4]{0:T(128)} %param.35) | copy-start | bytes 52
  0.6 169.1 %collective-permute-start = (bf16[2,32,128,512]{3,2,1,0:T(8,128)(2,1)}, bf16[2,32,128,512]{3,2,1,0:T(8,128)(2,1)}, u32[]{:S(2)}, u32[]{:S(2)}) collective-permute-start(bf16[2,32,128,512]{3,2,1,0:T(8,128)(2,1)} %here.2), channel_id=1, source_target_pairs={{0,1},{1,0},{2,3},{3,2},{4,5},{5,4},{6,7},{7,6},{8,9},{9,8},{10,11... | collective-permute-start | bytes 25165832 | tf_op jit(solution)/shard_map/ppermute | solution.py:737
  1.2 164.2 %collective-permute-start.1 = (bf16[2,2,128,512]{3,2,1,0:T(8,128)(2,1)}, bf16[2,2,128,512]{3,2,1,0:T(8,128)(2,1)}, u32[]{:S(2)}, u32[]{:S(2)}) collective-permute-start(bf16[2,2,128,512]{3,2,1,0:T(8,128)(2,1)} %here.3), channel_id=1, source_target_pairs={{0,1},{1,0},{2,3},{3,2},{4,5},{5,4},{6,7},{7,6},{8,9},{9,8},{10,11... | collective-permute-start | bytes 1572872 | tf_op jit(solution)/shard_map/ppermute | solution.py:737
  4.6 5.6 %copy-start.1 = (bf16[2,256,4096]{2,1,0:T(8,128)(2,1)S(1)}, bf16[2,256,4096]{2,1,0:T(8,128)(2,1)}, u32[]{:S(2)}) copy-start(bf16[2,256,4096]{2,1,0:T(8,128)(2,1)} %acts.3) | copy-start | bytes 12582916
  69.6 59.7 %copy-start.7 = (f32[2,32,16,128]{3,2,1,0:T(8,128)S(1)}, f32[2,32,16,128]{3,2,1,0:T(8,128)}, u32[]{:S(2)}) copy-start(f32[2,32,16,128]{3,2,1,0:T(8,128)} %param.28) | copy-start | bytes 1572868
  69.7 59.7 %copy-start.11 = (f32[2,2,32,16,128]{4,3,2,1,0:T(8,128)S(1)}, f32[2,2,32,16,128]{4,3,2,1,0:T(8,128)}, u32[]{:S(2)}) copy-start(f32[2,2,32,16,128]{4,3,2,1,0:T(8,128)} %param.29) | copy-start | bytes 3145732
  129.3 1.5 copy-start.12
  129.3 1.5 copy-start.16
  129.3 2.2 %copy-start.6 = (f32[2,2,256,256]{3,2,1,0:T(8,128)S(1)}, f32[2,2,256,256]{3,2,1,0:T(8,128)}, u32[]{:S(2)}) copy-start(f32[2,2,256,256]{3,2,1,0:T(8,128)} %param.27) | copy-start | bytes 3145732
  129.3 2.2 %copy-start.8 = (f32[2,256,256]{2,1,0:T(8,128)S(1)}, f32[2,256,256]{2,1,0:T(8,128)}, u32[]{:S(2)}) copy-start(f32[2,256,256]{2,1,0:T(8,128)} %param.26) | copy-start | bytes 1572868
  130.7 26.9 %copy-start.10 = (f32[2,32,16,128]{3,2,1,0:T(8,128)}, f32[2,32,16,128]{3,2,1,0:T(8,128)S(1)}, u32[]{:S(2)}) copy-start(f32[2,32,16,128]{3,2,1,0:T(8,128)S(1)} %get-tuple-element.24) | copy-start | bytes 1572868
  131.5 26.1 %copy-start.15 = (f32[2,2,16,128]{3,2,1,0:T(8,128)}, f32[2,2,16,128]{3,2,1,0:T(8,128)S(1)}, u32[]{:S(2)}) copy-start(f32[2,2,16,128]{3,2,1,0:T(8,128)S(1)} %get-tuple-element.29) | copy-start | bytes 98308
  131.9 25.7 %copy-start.9 = (f32[2,256,256]{2,1,0:T(8,128)}, f32[2,256,256]{2,1,0:T(8,128)S(1)}, u32[]{:S(2)}) copy-start(f32[2,256,256]{2,1,0:T(8,128)S(1)} %multiply_subtract_fusion.1) | copy-start | bytes 1572868
  157.7 7.5 %copy-start.17 = (s32[128]{0:T(128)S(1)}, s32[128]{0:T(128)}, u32[]{:S(2)}) copy-start(s32[128]{0:T(128)} %param.34) | copy-start | bytes 1540
  157.7 7.6 %copy-start.3 = (bf16[8,544,128]{2,1,0:T(8,128)(2,1)S(1)}, bf16[8,544,128]{2,1,0:T(8,128)(2,1)}, u32[]{:S(2)}) copy-start(bf16[8,544,128]{2,1,0:T(8,128)(2,1)} %get-tuple-element.15.up_here) | copy-start | bytes 3342340
  157.8 7.6 %copy-start.4 = (bf16[8,544,128]{2,1,0:T(8,128)(2,1)S(1)}, bf16[8,544,128]{2,1,0:T(8,128)(2,1)}, u32[]{:S(2)}) copy-start(bf16[8,544,128]{2,1,0:T(8,128)(2,1)} %get-tuple-element.16.up_there) | copy-start | bytes 3342340
  157.8 7.6 %copy-start.5 = (bf16[2,2,128,512]{3,2,1,0:T(8,128)(2,1)S(1)}, bf16[2,2,128,512]{3,2,1,0:T(8,128)(2,1)}, u32[]{:S(2)}) copy-start(bf16[2,2,128,512]{3,2,1,0:T(8,128)(2,1)} %here.3) | copy-start | bytes 1572868
  159.1 5.5 %copy-start.13 = (f32[1,2,2,16,128]{4,3,2,1,0:T(8,128)S(1)}, f32[1,2,2,16,128]{4,3,2,1,0:T(8,128)}, u32[]{:S(2)}) copy-start(f32[1,2,2,16,128]{4,3,2,1,0:T(8,128)} %get-tuple-element.27) | copy-start | bytes 98308
  159.1 5.5 %copy-start.14 = (f32[1,2,2,16,128]{4,3,2,1,0:T(8,128)S(1)}, f32[1,2,2,16,128]{4,3,2,1,0:T(8,128)}, u32[]{:S(2)}) copy-start(f32[1,2,2,16,128]{4,3,2,1,0:T(8,128)} %get-tuple-element.28) | copy-start | bytes 98308
  169.7 3.4 %copy-start.2 = (bf16[2,32,128,512]{3,2,1,0:T(8,128)(2,1)S(1)}, bf16[2,32,128,512]{3,2,1,0:T(8,128)(2,1)}, u32[]{:S(2)}) copy-start(bf16[2,32,128,512]{3,2,1,0:T(8,128)(2,1)} %here.2) | copy-start | bytes 25165828
